TPU v7x, 128 devices: a whole 4x4x4 slice. The times are simulated.
128 devices in a mesh: space: 16 (over z, y), member: 8 (over x, core).
Axes of the slice: x: 4, y: 4, z: 4, core: 2. Of those that a mesh axis runs over, the one named last changes fastest.
Arguments:
- residual: float32 [512, 512, 512], P('space', 'member'), may hold values from -8 to 8
- mobility: float32 [512, 512, 512], P('space', 'member'), may hold values from 0.1 to 10
- initial_guess: float32 [512, 512, 512], P('space', 'member'), may hold values from -4 to 4
Outputs:
- correction: float32 [512, 512, 512], P('space', 'member')
All inputs are finite; a program needn't handle non-finite values.
Results may differ from a plain program's by a relative error of at most 0.00002.
Values sent between devices are 32-bit elements; how exact they have to be, the bound alone decides.
No kernel may reach another device: no remote copies, remote signals or barrier semaphores. Data moves between devices by JAX's collectives and lax.ppermute only.
A program may use at most 192 MiB of HBM per device.

v0:
```python
import math

import jax
import jax.numpy as jnp
from jax import lax
from jax.sharding import PartitionSpec as P

sweep_weights = tuple((1.0 / (1.15 + 0.85 * math.cos(math.pi * (2 * j - 1) / 4.0)) for j in (1, 2)))


def extended(cells, sides, width):
    for axis, dim in sides:
        count = lax.axis_size(axis)
        ends = count - 1
        head = lax.slice_in_dim(cells, 0, width, axis=dim)
        tail = lax.slice_in_dim(cells, cells.shape[dim] - width, cells.shape[dim], axis=dim)
        cells = jnp.concatenate(
            [
                lax.ppermute(tail, axis, [(i, (i + 1) % count) for i in range(ends)]),
                cells,
                lax.ppermute(head, axis, [((i + 1) % count, i) for i in range(ends)]),
            ],
            axis=dim,
        )
    return cells


def neighbours(padded):
    return [
        padded[2:, 1:-1, 1:-1],
        padded[:-2, 1:-1, 1:-1],
        padded[1:-1, 2:, 1:-1],
        padded[1:-1, :-2, 1:-1],
        padded[1:-1, 1:-1, 2:],
        padded[1:-1, 1:-1, :-2],
    ]


def face_terms(padded_mob):
    center = padded_mob[1:-1, 1:-1, 1:-1]
    return [0.5 * (center + other) for other in neighbours(padded_mob)]


def sweep(padded_field, field, rhs, coeffs, diag, weight):
    flux = jnp.zeros_like(field)
    for coef, other in zip(coeffs, neighbours(padded_field)):
        flux = flux + coef * other
    image = diag * field - flux
    return field + weight * (rhs - image) / diag


def zpad(field):
    return jnp.pad(field, ((0, 0), (0, 0), (1, 1)))


def shards(residual, mobility, initial_guess):
    padded_mob = zpad(extended(mobility, (("space", 0), ("member", 1)), 1))
    coeffs = face_terms(padded_mob)
    diag = coeffs[0] + coeffs[1] + coeffs[2] + coeffs[3] + coeffs[4] + coeffs[5]
    field = initial_guess
    for weight in sweep_weights:
        padded = zpad(extended(field, (("space", 0), ("member", 1)), 1))
        field = sweep(padded, field, residual, coeffs, diag, weight)
    return field


def solution(mesh):
    placed = (P("space", "member", None), P("space", "member", None), P("space", "member", None))
    return jax.shard_map(
        shards, mesh=mesh, in_specs=placed, out_specs=P("space", "member", None), check_vma=False
    )
```

profile of v0, /device:TPU:33, one launch (start us, length us, event | category | flops | bytes accessed | tf_op | source)
XLA Modules:
  0.0 127.5 jit_solution(8769235151572790501)
XLA Ops:
  0.0 1.0 fusion.40
  1.0 3.2 %collective-permute-start.1 = (f32[1,64,512]{2,1,0:T(8,128)S(1)}, f32[1,64,512]{2,1,0:T(8,128)S(1)}, u32[]{:S(2)}, u32[]{:S(2)}) collective-permute-start(f32[1,64,512]{2,1,0:T(8,128)S(1)} %get-tuple-element.13), channel_id=1, source_target_pairs={{0,8},{8,16},{16,24},{24,32},{32,40},{40,48},{48,56},{56,64},{64,7... | collective-permute-start | bytes 393224 | tf_op jit(solution)/shard_map/ppermute | solution.py:19
  4.2 4.2 %collective-permute-start = (f32[1,64,512]{2,1,0:T(8,128)S(1)}, f32[1,64,512]{2,1,0:T(8,128)S(1)}, u32[]{:S(2)}, u32[]{:S(2)}) collective-permute-start(f32[1,64,512]{2,1,0:T(8,128)S(1)} %get-tuple-element.14), channel_id=1, source_target_pairs={{8,0},{16,8},{24,16},{32,24},{40,32},{48,40},{56,48},{64,56},{72,6... | collective-permute-start | bytes 393224 | tf_op jit(solution)/shard_map/ppermute | solution.py:21
  8.4 1.0 fusion.41
  9.4 1.9 %collective-permute-start.5 = (f32[1,64,512]{2,1,0:T(8,128)S(1)}, f32[1,64,512]{2,1,0:T(8,128)S(1)}, u32[]{:S(2)}, u32[]{:S(2)}) collective-permute-start(f32[1,64,512]{2,1,0:T(8,128)S(1)} %get-tuple-element.15), channel_id=1, source_target_pairs={{0,8},{8,16},{16,24},{24,32},{32,40},{40,48},{48,56},{56,64},{64,7... | collective-permute-start | bytes 393224 | tf_op jit(solution)/shard_map/ppermute | solution.py:19
  11.3 5.7 %collective-permute-start.4 = (f32[1,64,512]{2,1,0:T(8,128)S(1)}, f32[1,64,512]{2,1,0:T(8,128)S(1)}, u32[]{:S(2)}, u32[]{:S(2)}) collective-permute-start(f32[1,64,512]{2,1,0:T(8,128)S(1)} %get-tuple-element.16), channel_id=1, source_target_pairs={{8,0},{16,8},{24,16},{32,24},{40,32},{48,40},{56,48},{64,56},{72,6... | collective-permute-start | bytes 393224 | tf_op jit(solution)/shard_map/ppermute | solution.py:21
  17.1 4.6 %copy.27 = f32[32,64,512]{2,0,1:T(8,128)S(1)} copy(f32[32,64,512]{2,1,0:T(8,128)} %param.4) | data formatting | bytes 8388608 | tf_op args[1]
  21.7 2.4 %copy.47 = f32[32,64,512]{2,0,1:T(8,128)S(1)} copy(f32[32,64,512]{2,1,0:T(8,128)S(1)} %copy-done.1) | data formatting | bytes 8388608 | tf_op args[2]
  24.2 0.1 copy.28
  24.3 0.1 copy.26
  24.5 4.8 %collective-permute-start.3 = (f32[34,1,512]{2,0,1:T(8,128)S(1)}, f32[34,1,512]{2,0,1:T(8,128)S(1)}, u32[]{:S(2)}, u32[]{:S(2)}) collective-permute-start(f32[34,1,512]{2,0,1:T(8,128)S(1)} %get-tuple-element.7), channel_id=1, source_target_pairs={{0,1},{1,2},{2,3},{3,4},{4,5},{5,6},{6,7},{8,9},{9,10},{10,11},{11... | collective-permute-start | bytes 208904 | tf_op jit(solution)/shard_map/ppermute | solution.py:19
  29.3 1.9 %collective-permute-start.2 = (f32[34,1,512]{2,0,1:T(8,128)S(1)}, f32[34,1,512]{2,0,1:T(8,128)S(1)}, u32[]{:S(2)}, u32[]{:S(2)}) collective-permute-start(f32[34,1,512]{2,0,1:T(8,128)S(1)} %get-tuple-element.8), channel_id=1, source_target_pairs={{1,0},{2,1},{3,2},{4,3},{5,4},{6,5},{7,6},{9,8},{10,9},{11,10},{12... | collective-permute-start | bytes 208904 | tf_op jit(solution)/shard_map/ppermute | solution.py:21
  31.2 0.1 copy.41
  31.4 0.1 copy.40
  31.6 3.6 %collective-permute-start.7 = (f32[34,1,512]{2,0,1:T(8,128)S(1)}, f32[34,1,512]{2,0,1:T(8,128)S(1)}, u32[]{:S(2)}, u32[]{:S(2)}) collective-permute-start(f32[34,1,512]{2,0,1:T(8,128)S(1)} %get-tuple-element.9), channel_id=1, source_target_pairs={{0,1},{1,2},{2,3},{3,4},{4,5},{5,6},{6,7},{8,9},{9,10},{10,11},{11... | collective-permute-start | bytes 208904 | tf_op jit(solution)/shard_map/ppermute | solution.py:19
  35.2 2.1 %collective-permute-start.6 = (f32[34,1,512]{2,0,1:T(8,128)S(1)}, f32[34,1,512]{2,0,1:T(8,128)S(1)}, u32[]{:S(2)}, u32[]{:S(2)}) collective-permute-start(f32[34,1,512]{2,0,1:T(8,128)S(1)} %get-tuple-element.10), channel_id=1, source_target_pairs={{1,0},{2,1},{3,2},{4,3},{5,4},{6,5},{7,6},{9,8},{10,9},{11,10},{12... | collective-permute-start | bytes 208904 | tf_op jit(solution)/shard_map/ppermute | solution.py:21
  37.4 5.8 %select_maximum_fusion.8 = f32[34,66,514]{2,0,1:T(8,128)S(1)} fusion(f32[34,1,512]{2,0,1:T(8,128)S(1)} %collective-permute-done.2, f32[34,1,512]{2,0,1:T(8,128)S(1)} %collective-permute-done.3, f32[1,64,512]{2,0,1:T(1,128)S(1)} %copy.26, f32[32,64,512]{2,0,1:T(8,128)S(1)} %copy.27, f32[1,64,512]{2,0,1:T(1,128)S(1)} %copy.28), kind=kLoop, calls=%fused_computation.10 | loop fusion | flops 13840992 | bytes 9209376 | tf_op jit(solution)/shard_map/concatenate | solution.py:17
  43.2 7.5 %select_maximum_fusion.4 = f32[34,66,514]{2,0,1:T(8,128)} fusion(f32[34,1,512]{2,0,1:T(8,128)S(1)} %collective-permute-done.6, f32[34,1,512]{2,0,1:T(8,128)S(1)} %collective-permute-done.7, f32[1,64,512]{2,0,1:T(1,128)S(1)} %copy.40, f32[32,64,512]{2,0,1:T(8,128)S(1)} %copy.47, f32[1,64,512]{2,0,1:T(1,128)S(1)} %copy.41), kind=kLoop, calls=%fused_computation.6 | loop fusion | flops 13840992 | bytes 9209376 | tf_op jit(solution)/shard_map/concatenate | solution.py:17
  50.8 22.6 %fusion.20 = f32[32,64,512]{2,0,1:T(8,128)S(1)} fusion(f32[32,64,512]{2,0,1:T(8,128)} %copy-done, f32[34,66,514]{2,0,1:T(8,128)} %select_maximum_fusion.4, f32[34,1,512]{2,0,1:T(8,128)S(1)} %collective-permute-done.7, f32[1,64,512]{2,0,1:T(1,128)S(1)} %copy.40, f32[1,64,512]{2,0,1:T(1,128)S(1)} %copy.41, f32[34,1,512]{2,0,1:T(8,128)S(1)} %collective-permute-done.6, ...), kind=kLoop, calls=%fused_computation.45 | loop fusion | flops 52428800 | bytes 34357248 | tf_op jit(solution)/shard_map/add | solution.py:49
  73.4 0.2 fusion.39
  73.7 1.9 %collective-permute-start.8 = (f32[1,64,512]{2,1,0:T(8,128)S(1)}, f32[1,64,512]{2,1,0:T(8,128)S(1)}, u32[]{:S(2)}, u32[]{:S(2)}) collective-permute-start(f32[1,64,512]{2,1,0:T(8,128)S(1)} %copy.48), channel_id=1, source_target_pairs={{8,0},{16,8},{24,16},{32,24},{40,32},{48,40},{56,48},{64,56},{72,6... | collective-permute-start | bytes 393224 | tf_op jit(solution)/shard_map/ppermute | solution.py:21
  75.6 3.4 %collective-permute-start.9 = (f32[1,64,512]{2,1,0:T(8,128)S(1)}, f32[1,64,512]{2,1,0:T(8,128)S(1)}, u32[]{:S(2)}, u32[]{:S(2)}) collective-permute-start(f32[1,64,512]{2,1,0:T(8,128)S(1)} %copy.50), channel_id=1, source_target_pairs={{0,8},{8,16},{16,24},{24,32},{32,40},{40,48},{48,56},{56,64},{64,7... | collective-permute-start | bytes 393224 | tf_op jit(solution)/shard_map/ppermute | solution.py:19
  79.0 0.4 collective-permute-done.8
  79.4 0.1 copy.49
  79.5 3.9 %collective-permute-done.9 = f32[1,64,512]{2,1,0:T(8,128)S(1)} collective-permute-done((f32[1,64,512]{2,1,0:T(8,128)S(1)}, f32[1,64,512]{2,1,0:T(8,128)S(1)}, u32[]{:S(2)}, u32[]{:S(2)}) %collective-permute-start.9) | collective-permute-done | bytes 131104 | tf_op jit(solution)/shard_map/ppermute | solution.py:19
  83.4 0.1 copy.51
  83.6 5.1 %collective-permute-start.11 = (f32[34,1,512]{2,0,1:T(8,128)S(1)}, f32[34,1,512]{2,0,1:T(8,128)S(1)}, u32[]{:S(2)}, u32[]{:S(2)}) collective-permute-start(f32[34,1,512]{2,0,1:T(8,128)S(1)} %get-tuple-element.5), channel_id=1, source_target_pairs={{0,1},{1,2},{2,3},{3,4},{4,5},{5,6},{6,7},{8,9},{9,10},{10,11},{11... | collective-permute-start | bytes 208904 | tf_op jit(solution)/shard_map/ppermute | solution.py:19
  88.7 2.1 %collective-permute-start.10 = (f32[34,1,512]{2,0,1:T(8,128)S(1)}, f32[34,1,512]{2,0,1:T(8,128)S(1)}, u32[]{:S(2)}, u32[]{:S(2)}) collective-permute-start(f32[34,1,512]{2,0,1:T(8,128)S(1)} %get-tuple-element.6), channel_id=1, source_target_pairs={{1,0},{2,1},{3,2},{4,3},{5,4},{6,5},{7,6},{9,8},{10,9},{11,10},{12... | collective-permute-start | bytes 208904 | tf_op jit(solution)/shard_map/ppermute | solution.py:21
  90.9 3.6 %collective-permute-done.10 = f32[34,1,512]{2,0,1:T(8,128)S(1)} collective-permute-done((f32[34,1,512]{2,0,1:T(8,128)S(1)}, f32[34,1,512]{2,0,1:T(8,128)S(1)}, u32[]{:S(2)}, u32[]{:S(2)}) %collective-permute-start.10) | collective-permute-done | bytes 69664 | tf_op jit(solution)/shard_map/ppermute | solution.py:21
  94.5 7.5 %select_maximum_fusion = f32[34,66,514]{2,0,1:T(8,128)} fusion(f32[34,1,512]{2,0,1:T(8,128)S(1)} %collective-permute-done.10, f32[34,1,512]{2,0,1:T(8,128)S(1)} %collective-permute-done.11, f32[1,64,512]{2,0,1:T(1,128)S(1)} %copy.49, f32[32,64,512]{2,0,1:T(8,128)S(1)} %fusion.20, f32[1,64,512]{2,0,1:T(1,128)S(1)} %copy.51), kind=kLoop, calls=%fused_computation.2 | loop fusion | flops 13840992 | bytes 9209376 | tf_op jit(solution)/shard_map/concatenate | solution.py:17
  102.0 18.9 %fusion.6 = f32[32,64,512]{2,0,1:T(8,128)} fusion(f32[32,64,512]{2,0,1:T(8,128)S(1)} %fusion.20, f32[34,66,514]{2,0,1:T(8,128)} %select_maximum_fusion, f32[34,1,512]{2,0,1:T(8,128)S(1)} %collective-permute-done.11, f32[1,64,512]{2,0,1:T(1,128)S(1)} %copy.49, f32[1,64,512]{2,0,1:T(1,128)S(1)} %copy.51, f32[34,1,512]{2,0,1:T(8,128)S(1)} %collective-permute-done.10, ...), kind=kLoop, calls=%fused_computation.21 | loop fusion | flops 52428800 | bytes 34357248 | tf_op jit(solution)/shard_map/add | solution.py:49
  120.9 6.6 %copy.55 = f32[32,64,512]{2,1,0:T(8,128)} copy(f32[32,64,512]{2,0,1:T(8,128)} %fusion.6) | data formatting | bytes 8388608 | tf_op jit(solution)/shard_map/add | solution.py:49
  (18 shorter events, 0.1 us)
Async XLA Ops:
  1.0 23.2 %collective-permute-start.1 = (f32[1,64,512]{2,1,0:T(8,128)S(1)}, f32[1,64,512]{2,1,0:T(8,128)S(1)}, u32[]{:S(2)}, u32[]{:S(2)}) collective-permute-start(f32[1,64,512]{2,1,0:T(8,128)S(1)} %get-tuple-element.13), channel_id=1, source_target_pairs={{0,8},{8,16},{16,24},{24,32},{32,40},{40,48},{48,56},{56,64},{64,7... | collective-permute-start | bytes 393224 | tf_op jit(solution)/shard_map/ppermute | solution.py:19
  4.2 20.1 %collective-permute-start = (f32[1,64,512]{2,1,0:T(8,128)S(1)}, f32[1,64,512]{2,1,0:T(8,128)S(1)}, u32[]{:S(2)}, u32[]{:S(2)}) collective-permute-start(f32[1,64,512]{2,1,0:T(8,128)S(1)} %get-tuple-element.14), channel_id=1, source_target_pairs={{8,0},{16,8},{24,16},{32,24},{40,32},{48,40},{56,48},{64,56},{72,6... | collective-permute-start | bytes 393224 | tf_op jit(solution)/shard_map/ppermute | solution.py:21
  9.4 21.8 %collective-permute-start.5 = (f32[1,64,512]{2,1,0:T(8,128)S(1)}, f32[1,64,512]{2,1,0:T(8,128)S(1)}, u32[]{:S(2)}, u32[]{:S(2)}) collective-permute-start(f32[1,64,512]{2,1,0:T(8,128)S(1)} %get-tuple-element.15), channel_id=1, source_target_pairs={{0,8},{8,16},{16,24},{24,32},{32,40},{40,48},{48,56},{56,64},{64,7... | collective-permute-start | bytes 393224 | tf_op jit(solution)/shard_map/ppermute | solution.py:19
  11.3 10.4 %copy-start.1 = (f32[32,64,512]{2,1,0:T(8,128)S(1)}, f32[32,64,512]{2,1,0:T(8,128)}, u32[]{:S(2)}) copy-start(f32[32,64,512]{2,1,0:T(8,128)} %param.5) | copy-start | bytes 12582916
  11.3 20.1 %collective-permute-start.4 = (f32[1,64,512]{2,1,0:T(8,128)S(1)}, f32[1,64,512]{2,1,0:T(8,128)S(1)}, u32[]{:S(2)}, u32[]{:S(2)}) collective-permute-start(f32[1,64,512]{2,1,0:T(8,128)S(1)} %get-tuple-element.16), channel_id=1, source_target_pairs={{8,0},{16,8},{24,16},{32,24},{40,32},{48,40},{56,48},{64,56},{72,6... | collective-permute-start | bytes 393224 | tf_op jit(solution)/shard_map/ppermute | solution.py:21
  24.1 19.1 %copy-start = (f32[32,64,512]{2,0,1:T(8,128)}, f32[32,64,512]{2,0,1:T(8,128)S(1)}, u32[]{:S(2)}) copy-start(f32[32,64,512]{2,0,1:T(8,128)S(1)} %copy.47) | copy-start | bytes 12582916
  24.5 12.8 %collective-permute-start.3 = (f32[34,1,512]{2,0,1:T(8,128)S(1)}, f32[34,1,512]{2,0,1:T(8,128)S(1)}, u32[]{:S(2)}, u32[]{:S(2)}) collective-permute-start(f32[34,1,512]{2,0,1:T(8,128)S(1)} %get-tuple-element.7), channel_id=1, source_target_pairs={{0,1},{1,2},{2,3},{3,4},{4,5},{5,6},{6,7},{8,9},{9,10},{10,11},{11... | collective-permute-start | bytes 208904 | tf_op jit(solution)/shard_map/ppermute | solution.py:19
  29.3 8.0 %collective-permute-start.2 = (f32[34,1,512]{2,0,1:T(8,128)S(1)}, f32[34,1,512]{2,0,1:T(8,128)S(1)}, u32[]{:S(2)}, u32[]{:S(2)}) collective-permute-start(f32[34,1,512]{2,0,1:T(8,128)S(1)} %get-tuple-element.8), channel_id=1, source_target_pairs={{1,0},{2,1},{3,2},{4,3},{5,4},{6,5},{7,6},{9,8},{10,9},{11,10},{12... | collective-permute-start | bytes 208904 | tf_op jit(solution)/shard_map/ppermute | solution.py:21
  31.6 11.6 %collective-permute-start.7 = (f32[34,1,512]{2,0,1:T(8,128)S(1)}, f32[34,1,512]{2,0,1:T(8,128)S(1)}, u32[]{:S(2)}, u32[]{:S(2)}) collective-permute-start(f32[34,1,512]{2,0,1:T(8,128)S(1)} %get-tuple-element.9), channel_id=1, source_target_pairs={{0,1},{1,2},{2,3},{3,4},{4,5},{5,6},{6,7},{8,9},{9,10},{10,11},{11... | collective-permute-start | bytes 208904 | tf_op jit(solution)/shard_map/ppermute | solution.py:19
  35.2 8.0 %collective-permute-start.6 = (f32[34,1,512]{2,0,1:T(8,128)S(1)}, f32[34,1,512]{2,0,1:T(8,128)S(1)}, u32[]{:S(2)}, u32[]{:S(2)}) collective-permute-start(f32[34,1,512]{2,0,1:T(8,128)S(1)} %get-tuple-element.10), channel_id=1, source_target_pairs={{1,0},{2,1},{3,2},{4,3},{5,4},{6,5},{7,6},{9,8},{10,9},{11,10},{12... | collective-permute-start | bytes 208904 | tf_op jit(solution)/shard_map/ppermute | solution.py:21
  73.7 5.7 %collective-permute-start.8 = (f32[1,64,512]{2,1,0:T(8,128)S(1)}, f32[1,64,512]{2,1,0:T(8,128)S(1)}, u32[]{:S(2)}, u32[]{:S(2)}) collective-permute-start(f32[1,64,512]{2,1,0:T(8,128)S(1)} %copy.48), channel_id=1, source_target_pairs={{8,0},{16,8},{24,16},{32,24},{40,32},{48,40},{56,48},{64,56},{72,6... | collective-permute-start | bytes 393224 | tf_op jit(solution)/shard_map/ppermute | solution.py:21
  75.6 7.8 %collective-permute-start.9 = (f32[1,64,512]{2,1,0:T(8,128)S(1)}, f32[1,64,512]{2,1,0:T(8,128)S(1)}, u32[]{:S(2)}, u32[]{:S(2)}) collective-permute-start(f32[1,64,512]{2,1,0:T(8,128)S(1)} %copy.50), channel_id=1, source_target_pairs={{0,8},{8,16},{16,24},{24,32},{32,40},{40,48},{48,56},{56,64},{64,7... | collective-permute-start | bytes 393224 | tf_op jit(solution)/shard_map/ppermute | solution.py:19
  83.6 7.2 %collective-permute-start.11 = (f32[34,1,512]{2,0,1:T(8,128)S(1)}, f32[34,1,512]{2,0,1:T(8,128)S(1)}, u32[]{:S(2)}, u32[]{:S(2)}) collective-permute-start(f32[34,1,512]{2,0,1:T(8,128)S(1)} %get-tuple-element.5), channel_id=1, source_target_pairs={{0,1},{1,2},{2,3},{3,4},{4,5},{5,6},{6,7},{8,9},{9,10},{10,11},{11... | collective-permute-start | bytes 208904 | tf_op jit(solution)/shard_map/ppermute | solution.py:19
  88.7 5.8 %collective-permute-start.10 = (f32[34,1,512]{2,0,1:T(8,128)S(1)}, f32[34,1,512]{2,0,1:T(8,128)S(1)}, u32[]{:S(2)}, u32[]{:S(2)}) collective-permute-start(f32[34,1,512]{2,0,1:T(8,128)S(1)} %get-tuple-element.6), channel_id=1, source_target_pairs={{1,0},{2,1},{3,2},{4,3},{5,4},{6,5},{7,6},{9,8},{10,9},{11,10},{12... | collective-permute-start | bytes 208904 | tf_op jit(solution)/shard_map/ppermute | solution.py:21
where the time goes:
time: 128 us; the launch traced here: 127 us
  other arithmetic  62.5 us (49%)
  starting transfers between devices  40 us (31%)
  local copies, waits for them, and re-layouts  16.8 us (13%)
  waiting for transfers between devices  7.95 us (6%)
    add x2, other arithmetic, sweep(): return field + weight * (rhs - image) / diag  41.5 us
    ppermute x6, starting transfers between devices, extended(): lax.ppermute(tail, axis, [(i, (i + 1) % count) for i in range(ends)])  22 us
    concatenate x6, other arithmetic, extended(): jnp.concatenate([lax.ppermute(tail, axis, [(i, (i + 1) % count) for i in...  21 us
    ppermute x6, starting transfers between devices, extended(): lax.ppermute(head, axis, [((i + 1) % count, i) for i in range(ends)])  18 us
    unnamed x6, local copies, waits for them, and re-layouts  7.06 us
    add x1, local copies, waits for them, and re-layouts, sweep(): return field + weight * (rhs - image) / diag  6.63 us
    ppermute x6, waiting for transfers between devices, extended(): lax.ppermute(head, axis, [((i + 1) % count, i) for i in range(ends)])  4.02 us
    ppermute x6, waiting for transfers between devices, extended(): lax.ppermute(tail, axis, [(i, (i + 1) % count) for i in range(ends)])  3.93 us
  transfers between devices with their start and end apart: 12, of which 3 were waited for; matrix products, arithmetic and copies ran while one was open for 11% of the time, Pallas kernels for 0%

commit v1 on v0

v1 whole, which is shorter than its diff:
```python
import math

import jax
import jax.numpy as jnp
from jax import lax
from jax.experimental import pallas as pl
from jax.experimental.pallas import tpu as pltpu
from jax.sharding import PartitionSpec as P

sweep_weights = tuple((1.0 / (1.15 + 0.85 * math.cos(math.pi * (2 * j - 1) / 4.0)) for j in (1, 2)))

LANES = 128
RING = 4
ROWS = 8
VMEM = pl.BlockSpec(memory_space=pltpu.VMEM)
HBM = pl.BlockSpec(memory_space=pltpu.HBM)
F32 = jnp.float32


def lane_slices(nz):
    return [slice(k * LANES, (k + 1) * LANES) for k in range(nz // LANES)]


def iotas():
    row = lax.broadcasted_iota(jnp.int32, (ROWS, LANES), 0)
    lane = lax.broadcasted_iota(jnp.int32, (ROWS, LANES), 1)
    return row, lane


class Slab:
    def __init__(self, fields, rings, row_ok):
        self.e, self.m, self.r = fields
        self.cx, self.cy, self.cz, self.rt, self.e1 = rings
        self.strips = self.cx.shape[1] // ROWS - 1
        self.tiles = lane_slices(self.cx.shape[2])
        self.row_ok = row_ok
        row, lane = iotas()
        self.first_row, self.last_row = row == 0, row == ROWS - 1
        self.first_lane, self.last_lane = lane == 0, lane == LANES - 1

    def slot(self, i):
        return (i + RING) % RING if isinstance(i, int) else lax.rem(i, RING)

    def get(self, field, i, j):
        plane, halo = field(i)
        ref, at = halo if j == self.strips else plane
        first = 0 if j == self.strips else ROWS * j
        return [ref[at, first : first + ROWS, s] for s in self.tiles]

    def ring(self, ref, i, j):
        return [ref[i, ROWS * j : ROWS * (j + 1), s] for s in self.tiles]

    def put(self, ref, i, j, vals):
        for s, v in zip(self.tiles, vals):
            ref[i, ROWS * j : ROWS * (j + 1), s] = v

    def roll_up(self, vals):
        return [pltpu.roll(v, ROWS - 1, 0) for v in vals]

    def roll_down(self, vals):
        return [pltpu.roll(v, 1, 0) for v in vals]

    def next_rows(self, here, there):
        return [jnp.where(self.last_row, b, a) for a, b in zip(here, there)]

    def prev_rows(self, here, there):
        return [jnp.where(self.first_row, b, a) for a, b in zip(here, there)]

    def next_lanes(self, vals):
        turned = [pltpu.roll(v, LANES - 1, 1) for v in vals]
        return [jnp.where(self.last_lane, b, a) for a, b in zip(turned, turned[1:] + [0.0])]

    def prev_lanes(self, vals):
        turned = [pltpu.roll(v, 1, 1) for v in vals]
        return [jnp.where(self.first_lane, b, a) for a, b in zip(turned, [0.0] + turned[:-1])]

    def first(self, i, halo_strip=True, keep=None):
        w = sweep_weights[0]
        n = self.strips
        last = n if halo_strip else n - 1
        cur, prev = self.slot(i), self.slot(i - 1)

        def load(j):
            e = self.get(self.e, i, j)
            m = self.get(self.m, i, j)
            return e, m, self.roll_up(e), self.roll_up(m), [f(v) for v in (e, m) for f in (self.next_lanes, self.prev_lanes)]

        e, m = self.get(self.e, i, n), self.get(self.m, i, n)
        top = here = load(0)
        cy = [a + b for a, b in zip(m, self.next_rows(self.roll_up(m), top[3]))]
        cyd = self.roll_down(cy)
        gd = self.roll_down([a * b for a, b in zip(cy, e)])
        for j in range(last + 1):
            there = load(j + 1) if j < n else top
            e, m, eu, mu, (e_zp, e_zm, m_zp, m_zm) = here
            cy = [a + b for a, b in zip(m, self.next_rows(mu, there[3]))]
            cyd_j = self.roll_down(cy)
            gd_j = self.roll_down([a * b for a, b in zip(cy, e)])
            cy_dn, g_dn = self.prev_rows(cyd_j, cyd), self.prev_rows(gd_j, gd)
            e_up = self.next_rows(eu, there[2])
            exm = self.get(self.e, i - 1, j)
            exp = self.get(self.e, i + 1, j)
            mxp = self.get(self.m, i + 1, j)
            r = self.get(self.r, i, j)
            cxm = self.ring(self.cx, prev, j)
            keeps = [[], [], [], [], []]
            for k in range(len(self.tiles)):
                cx = m[k] + mxp[k]
                cz, cz_dn = m[k] + m_zp[k], m[k] + m_zm[k]
                t = ((cx + cxm[k]) + (cy[k] + cy_dn[k])) + (cz + cz_dn)
                num = ((cx * exp[k] + cxm[k] * exm[k]) + (cy[k] * e_up[k] + g_dn[k])) + (
                    (cz * e_zp[k] + cz_dn * e_zm[k]) + (r[k] + r[k])
                )
                rt = 1.0 / t
                e1 = (1.0 - w) * e[k] + (w * rt) * num
                if j == n:
                    e1 = jnp.where(self.row_ok, e1, 0.0)
                if keep is not None:
                    e1 = jnp.where(keep, e1, 0.0)
                for vals, v in zip(keeps, (cx, cy[k], cz, rt, e1)):
                    vals.append(v)
            for ref, vals in zip((self.cx, self.cy, self.cz, self.rt, self.e1), keeps):
                if j < n or ref is self.cx or ref is self.cy or ref is self.e1:
                    self.put(ref, cur, j, vals)
            cyd, gd = cyd_j, gd_j
            here = there
            yield

    def faces_x(self, i, strips):
        for j in strips:
            m = self.get(self.m, i, j)
            mxp = self.get(self.m, i + 1, j)
            self.put(self.cx, self.slot(i), j, [a + b for a, b in zip(m, mxp)])

    def second(self, i, out, o):
        w = sweep_weights[1]
        n = self.strips
        cur, prev, nxt = self.slot(i), self.slot(i - 1), self.slot(i + 1)

        def load(j):
            e, cy = self.ring(self.e1, cur, j), self.ring(self.cy, cur, j)
            g = self.roll_down([a * b for a, b in zip(cy, e)])
            if j == n:
                return e, cy, g, self.roll_up(e)
            cz = self.ring(self.cz, cur, j)
            h = self.prev_lanes([a * b for a, b in zip(cz, e)])
            return e, cy, g, self.roll_up(e), cz, self.next_lanes(e), h

        gd = load(n)[2]
        here = load(0)
        for j in range(n):
            there = load(j + 1)
            e, cy, g, eu, cz, e_zp, h_dn = here
            e_up, g_dn = self.next_rows(eu, there[3]), self.prev_rows(g, gd)
            exm, exp = self.ring(self.e1, prev, j), self.ring(self.e1, nxt, j)
            cxm, cx = self.ring(self.cx, prev, j), self.ring(self.cx, cur, j)
            rt = self.ring(self.rt, cur, j)
            r = self.get(self.r, i, j)
            outs = []
            for k in range(len(self.tiles)):
                num = ((cx[k] * exp[k] + cxm[k] * exm[k]) + (cy[k] * e_up[k] + g_dn[k])) + (
                    (cz[k] * e_zp[k] + h_dn[k]) + (r[k] + r[k])
                )
                outs.append((1.0 - w) * e[k] + (w * rt[k]) * num)
            self.put(out, o, j, outs)
            here, gd = there, g
            yield


def run(*passes):
    passes = list(passes)
    while passes:
        passes = [p for p in passes if next(p, StopIteration) is not StopIteration]


def pairs(first, n):
    return [p for i in range(first, n - 1, 2) for p in ((i, i + 1), (i + 1, i))]


def is_even(axis):
    return lax.rem(lax.axis_index(axis), 2) == 0


def swap(x, axis, first):
    return lax.ppermute(x, axis, pairs(first, lax.axis_size(axis)))


def row_mask():
    me, last = lax.axis_index("member"), lax.axis_size("member") - 1
    row, _ = iotas()
    after = jnp.where(me < last, 1, 0)
    before = jnp.where(me > 0, 1, 0)
    return jnp.where(row < ROWS // 2, after, before) == 1


def rings(ny, nz):
    return [pltpu.VMEM((RING, ny + ROWS, nz), F32)] * 5


def turned(v, by):
    return pltpu.roll(v, by % ROWS, 0)


def send_kernel(e, m, r, to_row_even, to_row_odd, to_plane_even, to_plane_odd, top, bottom, sems, plane_sems):
    nx, ny, nz = e.shape
    reads = []
    for k, src in enumerate((e, m, r)):
        for dst, at in ((top, 0), (bottom, ny - ROWS)):
            reads.append(pltpu.make_async_copy(src.at[:, at : at + ROWS], dst.at[k], sems.at[len(reads)]))
    for c in reads:
        c.start()
    even = is_even("space")
    planes = []
    for dst, high in ((to_plane_even, even), (to_plane_odd, jnp.logical_not(even))):
        two, one = jnp.where(high, nx - 2, 0), jnp.where(high, nx - 1, 0)
        for src, dst_at, size, at in ((e, 0, 2, two), (m, 2, 2, two), (r, 4, 1, one)):
            planes.append(
                pltpu.make_async_copy(src.at[pl.ds(at, size)], dst.at[dst_at : dst_at + size], plane_sems.at[len(planes)])
            )
    for c in planes:
        c.start()
    for c in reads:
        c.wait()

    def fill(to_next, to_prev):
        row = lax.broadcasted_iota(jnp.int32, (ROWS, nz), 0)

        @pl.loop(0, nx)
        def _(i):
            to_next[i] = jnp.where(
                row >= ROWS - 2,
                bottom[0, i],
                jnp.where(row >= ROWS - 4, turned(bottom[1, i], -2), turned(bottom[2, i], -4)),
            )
            to_prev[i] = jnp.where(row < 2, top[0, i], jnp.where(row < 4, turned(top[1, i], 2), turned(top[2, i], 4)))

    @pl.when(is_even("member"))
    def _():
        fill(to_row_even, to_row_odd)

    @pl.when(jnp.logical_not(is_even("member")))
    def _():
        fill(to_row_odd, to_row_even)

    for c in planes:
        c.wait()


def send(e, m, r):
    nx, ny, nz = e.shape
    rows = jax.ShapeDtypeStruct((nx, ROWS, nz), F32)
    planes = jax.ShapeDtypeStruct((5, ny, nz), F32)
    strips = pltpu.VMEM((3, nx, ROWS, nz), F32)
    return pl.pallas_call(
        send_kernel,
        out_shape=[rows, rows, planes, planes],
        in_specs=[HBM] * 3,
        out_specs=[VMEM] * 4,
        scratch_shapes=[strips, strips, pltpu.SemaphoreType.DMA((6,)), pltpu.SemaphoreType.DMA((6,))],
        compiler_params=pltpu.CompilerParams(vmem_limit_bytes=16 * 2**20),
        name="send",
    )(e, m, r)


def halo_kernel(got_even, got_odd, eh, mh, rh, corner_even, corner_odd):
    nx, _, nz = eh.shape
    row = lax.broadcasted_iota(jnp.int32, (ROWS, nz), 0)
    after = row < ROWS // 2

    def fill(from_next, from_prev):
        @pl.loop(0, nx)
        def _(i):
            a, b = from_next[i], from_prev[i]
            eh[i] = jnp.where(after, a, b)
            mh[i] = jnp.where(after, turned(a, -2), turned(b, 2))
            rh[i] = jnp.where(after, turned(a, -4), turned(b, 4))

    @pl.when(is_even("member"))
    def _():
        fill(got_even, got_odd)

    @pl.when(jnp.logical_not(is_even("member")))
    def _():
        fill(got_odd, got_even)

    even = is_even("space")
    for dst, high in ((corner_even, even), (corner_odd, jnp.logical_not(even))):
        at = jnp.where(high, nx - 1, 0)
        dst[0] = eh[at]
        dst[1] = mh[at]


def halo(got_even, got_odd):
    nx, _, nz = got_even.shape
    strip = jax.ShapeDtypeStruct((nx, ROWS, nz), F32)
    corner = jax.ShapeDtypeStruct((2, ROWS, nz), F32)
    return pl.pallas_call(
        halo_kernel,
        out_shape=[strip] * 3 + [corner] * 2,
        in_specs=[VMEM] * 2,
        out_specs=[VMEM] * 5,
        compiler_params=pltpu.CompilerParams(vmem_limit_bytes=8 * 2**20),
        name="halo",
    )(got_even, got_odd)


def inner_kernel(e, m, r, eh, mh, rh, out_hbm, out, cx, cy, cz, rt, e1, sems):
    nx = e.shape[0]
    fields = [lambda i, own=own, strip=strip: ((own, i), (strip, i)) for own, strip in ((e, eh), (m, mh), (r, rh))]
    slab = Slab(fields, (cx, cy, cz, rt, e1), row_mask())

    def out_copy(i):
        return pltpu.make_async_copy(out.at[i], out_hbm.at[i], sems.at[i])

    slab.faces_x(0, range(slab.strips + 1))

    @pl.loop(1, 4)
    def _(i):
        run(slab.first(i))

    @pl.loop(4, nx - 1)
    def _(i):
        run(slab.second(i - 2, out, i - 2), slab.first(i))
        out_copy(i - 2).start()

    run(slab.second(nx - 3, out, nx - 3))
    out_copy(nx - 3).start()

    @pl.loop(2, nx - 2)
    def _(i):
        out_copy(i).wait()


def inner(e, m, r, eh, mh, rh):
    nx, ny, nz = e.shape
    return pl.pallas_call(
        inner_kernel,
        out_shape=jax.ShapeDtypeStruct((nx, ny, nz), F32),
        in_specs=[VMEM] * 6,
        out_specs=HBM,
        scratch_shapes=[pltpu.VMEM((nx, ny, nz), F32)] + rings(ny, nz) + [pltpu.SemaphoreType.DMA((nx,))],
        compiler_params=pltpu.CompilerParams(vmem_limit_bytes=16 * 2**20),
        cost_estimate=pl.CostEstimate(flops=70 * nx * ny * nz, bytes_accessed=16 * nx * ny * nz, transcendentals=0),
        name="inner",
    )(e, m, r, eh, mh, rh)


def outer_kernel(e, m, r, eh, mh, rh, got_even, got_odd, corner_even, corner_odd, _, out_hbm, out, cx, cy, cz, rt, e1, sems):
    nx = e.shape[0]
    me, count = lax.axis_index("space"), lax.axis_size("space")
    mask = row_mask()
    writes = []
    for side, (got, corner) in enumerate(((got_even, corner_even), (got_odd, corner_odd))):
        high = is_even("space") if side == 0 else jnp.logical_not(is_even("space"))

        def at(q, high=high):
            return jnp.where(high, nx - 1 - q, q)

        def field(k, own, strip, got=got, corner=corner, high=high, at=at):
            def find(q):
                if q >= 0:
                    return (own, at(q)), (strip, at(q))
                if k == 2:
                    return (got, 4), None
                return (got, 2 * k + jnp.where(high, -1 - q, 2 + q)), (corner, k)

            return find

        fields = [field(k, *refs) for k, refs in enumerate(((e, eh), (m, mh), (r, rh)))]
        slab = Slab(fields, (cx, cy, cz, rt, e1), mask)
        there = jnp.where(high, me < count - 1, me > 0)
        keep = jnp.broadcast_to(jnp.where(there, 1, 0), (ROWS, LANES)) == 1
        slab.faces_x(-2, range(slab.strips))
        slab.faces_x(-1, [slab.strips])
        run(slab.first(-1, halo_strip=False, keep=keep))
        run(slab.first(0))
        run(slab.first(1))
        run(slab.first(2))
        for q in (0, 1):
            run(slab.second(q, out, 2 * side + q))
            c = pltpu.make_async_copy(out.at[2 * side + q], out_hbm.at[at(q)], sems.at[2 * side + q])
            c.start()
            writes.append(c)
    for c in writes:
        c.wait()


def outer(e, m, r, eh, mh, rh, got_even, got_odd, corner_even, corner_odd, out):
    nx, ny, nz = e.shape
    return pl.pallas_call(
        outer_kernel,
        out_shape=jax.ShapeDtypeStruct((nx, ny, nz), F32),
        in_specs=[VMEM] * 10 + [HBM],
        out_specs=HBM,
        input_output_aliases={10: 0},
        scratch_shapes=[pltpu.VMEM((4, ny, nz), F32)] + rings(ny, nz) + [pltpu.SemaphoreType.DMA((4,))],
        compiler_params=pltpu.CompilerParams(vmem_limit_bytes=16 * 2**20),
        name="outer",
    )(e, m, r, eh, mh, rh, got_even, got_odd, corner_even, corner_odd, out)


def shards(residual, mobility, initial_guess):
    e, m, r = initial_guess, mobility, residual
    row_even, row_odd, plane_even, plane_odd = send(e, m, r)
    row_even = swap(row_even, "member", 0)
    row_odd = swap(row_odd, "member", 1)
    plane_even = swap(plane_even, "space", 0)
    plane_odd = swap(plane_odd, "space", 1)
    eh, mh, rh, corner_even, corner_odd = halo(row_even, row_odd)
    corner_even = swap(corner_even, "space", 0)
    corner_odd = swap(corner_odd, "space", 1)
    out = inner(e, m, r, eh, mh, rh)
    return outer(e, m, r, eh, mh, rh, plane_even, plane_odd, corner_even, corner_odd, out)


def solution(mesh):
    placed = P("space", "member", None)
    return jax.shard_map(shards, mesh=mesh, in_specs=(placed,) * 3, out_specs=placed, check_vma=False)
```

time: 128 us -> 44.1 us (0.34)
  the two profiles are of different devices: /device:TPU:33 before, /device:TPU:99 now
where the time goes in v1:
time: 44.1 us; the launch traced here: 43.9 us
  Pallas kernels  16.3 us (37%)
  starting transfers between devices  13.2 us (30%)
  waiting for transfers between devices  7.76 us (18%)
  local copies, waits for them, and re-layouts  6.56 us (15%)
    ppermute x6, starting transfers between devices, swap(): return lax.ppermute(x, axis, pairs(first, lax.axis_size(axis)))  13.2 us
    pallas_call x1, Pallas kernels, inner(): pl.pallas_call(inner_kernel, out_shape=jax.ShapeDtypeStruct((nx, ny, nz),...  12.1 us
    ppermute x6, waiting for transfers between devices, swap(): return lax.ppermute(x, axis, pairs(first, lax.axis_size(axis)))  7.76 us
    unnamed x6, local copies, waits for them, and re-layouts  6.56 us
    pallas_call x1, Pallas kernels, outer(): pl.pallas_call(outer_kernel, out_shape=jax.ShapeDtypeStruct((nx, ny, nz),...  2.85 us
    pallas_call x1, Pallas kernels, send(): pl.pallas_call(send_kernel, out_shape=[rows, rows, planes, planes], in_sp...  1.11 us
  transfers between devices with their start and end apart: 6, of which 1 were waited for; matrix products, arithmetic and copies ran while one was open for 0% of the time, Pallas kernels for 28%

profile of v1, /device:TPU:99, one launch (start us, length us, event | category | flops | bytes accessed | tf_op | source)
XLA Modules:
  0.0 43.9 jit_solution(11116257294096191958)
XLA Ops:
  0.0 0.0 copy-start
  0.0 2.2 %copy-done = f32[32,64,512]{2,1,0:T(8,128)S(1)} copy-done((f32[32,64,512]{2,1,0:T(8,128)S(1)}, f32[32,64,512]{2,1,0:T(8,128)}, u32[]{:S(2)}) %copy-start) | copy-done | bytes 4194328
  2.2 0.0 copy-start.1
  2.2 2.2 %copy-done.1 = f32[32,64,512]{2,1,0:T(8,128)S(1)} copy-done((f32[32,64,512]{2,1,0:T(8,128)S(1)}, f32[32,64,512]{2,1,0:T(8,128)}, u32[]{:S(2)}) %copy-start.1) | copy-done | bytes 4194328
  4.4 0.0 copy-start.2
  4.4 2.2 %copy-done.2 = f32[32,64,512]{2,1,0:T(8,128)S(1)} copy-done((f32[32,64,512]{2,1,0:T(8,128)S(1)}, f32[32,64,512]{2,1,0:T(8,128)}, u32[]{:S(2)}) %copy-start.2) | copy-done | bytes 4194328
  6.6 1.1 %send.1 = (f32[32,8,512]{2,1,0:T(8,128)S(1)}, f32[32,8,512]{2,1,0:T(8,128)S(1)}, f32[5,64,512]{2,1,0:T(8,128)S(1)}, f32[5,64,512]{2,1,0:T(8,128)S(1)}) custom-call(f32[32,64,512]{2,1,0:T(8,128)S(1)} %copy-done, f32[32,64,512]{2,1,0:T(8,128)S(1)} %copy-done.1, f32[32,64,512]{2,1,0:T(8,128)S(1)} %copy-done.2), custom_call_target="tpu_custom_call" | custom-call | tf_op jit(solution)/shard_map/send/pallas_call | solution.py:254
  7.7 1.4 %collective-permute-start.2 = (f32[5,64,512]{2,1,0:T(8,128)S(1)}, f32[5,64,512]{2,1,0:T(8,128)S(1)}, u32[]{:S(2)}, u32[]{:S(2)}) collective-permute-start(f32[5,64,512]{2,1,0:T(8,128)S(1)} %get-tuple-element.19), channel_id=1, source_target_pairs={{0,8},{8,0},{16,24},{24,16},{32,40},{40,32},{48,56},{56,48},{64,72... | collective-permute-start | bytes 1966088 | tf_op jit(solution)/shard_map/ppermute | solution.py:185
  9.1 3.6 %collective-permute-start.3 = (f32[5,64,512]{2,1,0:T(8,128)S(1)}, f32[5,64,512]{2,1,0:T(8,128)S(1)}, u32[]{:S(2)}, u32[]{:S(2)}) collective-permute-start(f32[5,64,512]{2,1,0:T(8,128)S(1)} %get-tuple-element.20), channel_id=1, source_target_pairs={{8,16},{16,8},{24,32},{32,24},{40,48},{48,40},{56,64},{64,56},{72,... | collective-permute-start | bytes 1966088 | tf_op jit(solution)/shard_map/ppermute | solution.py:185
  12.7 1.3 %collective-permute-start = (f32[32,8,512]{2,1,0:T(8,128)S(1)}, f32[32,8,512]{2,1,0:T(8,128)S(1)}, u32[]{:S(2)}, u32[]{:S(2)}) collective-permute-start(f32[32,8,512]{2,1,0:T(8,128)S(1)} %get-tuple-element.14), channel_id=1, source_target_pairs={{0,1},{1,0},{2,3},{3,2},{4,5},{5,4},{6,7},{7,6},{8,9},{9,8},{10,11... | collective-permute-start | bytes 1572872 | tf_op jit(solution)/shard_map/ppermute | solution.py:185
  14.0 3.0 %collective-permute-start.1 = (f32[32,8,512]{2,1,0:T(8,128)S(1)}, f32[32,8,512]{2,1,0:T(8,128)S(1)}, u32[]{:S(2)}, u32[]{:S(2)}) collective-permute-start(f32[32,8,512]{2,1,0:T(8,128)S(1)} %get-tuple-element.15), channel_id=1, source_target_pairs={{1,2},{2,1},{3,4},{4,3},{5,6},{6,5},{9,10},{10,9},{11,12},{12,11},... | collective-permute-start | bytes 1572872 | tf_op jit(solution)/shard_map/ppermute | solution.py:185
  17.0 0.0 collective-permute-done.got_even
  17.1 7.7 %collective-permute-done.1.got_odd = f32[32,8,512]{2,1,0:T(8,128)S(1)} collective-permute-done((f32[32,8,512]{2,1,0:T(8,128)S(1)}, f32[32,8,512]{2,1,0:T(8,128)S(1)}, u32[]{:S(2)}, u32[]{:S(2)}) %collective-permute-start.1) | collective-permute-done | bytes 524320 | tf_op jit(solution)/shard_map/ppermute | solution.py:185
  24.8 0.2 halo.1
  25.0 0.6 %collective-permute-start.4 = (f32[2,8,512]{2,1,0:T(8,128)S(1)}, f32[2,8,512]{2,1,0:T(8,128)S(1)}, u32[]{:S(2)}, u32[]{:S(2)}) collective-permute-start(f32[2,8,512]{2,1,0:T(8,128)S(1)} %get-tuple-element.21), channel_id=1, source_target_pairs={{0,8},{8,0},{16,24},{24,16},{32,40},{40,32},{48,56},{56,48},{64,72... | collective-permute-start | bytes 98312 | tf_op jit(solution)/shard_map/ppermute | solution.py:185
  25.7 3.2 %collective-permute-start.5 = (f32[2,8,512]{2,1,0:T(8,128)S(1)}, f32[2,8,512]{2,1,0:T(8,128)S(1)}, u32[]{:S(2)}, u32[]{:S(2)}) collective-permute-start(f32[2,8,512]{2,1,0:T(8,128)S(1)} %get-tuple-element.22), channel_id=1, source_target_pairs={{8,16},{16,8},{24,32},{32,24},{40,48},{48,40},{56,64},{64,56},{72,... | collective-permute-start | bytes 98312 | tf_op jit(solution)/shard_map/ppermute | solution.py:185
  28.9 12.1 %inner.1._ = f32[32,64,512]{2,1,0:T(8,128)} custom-call(f32[32,64,512]{2,1,0:T(8,128)S(1)} %copy-done, f32[32,64,512]{2,1,0:T(8,128)S(1)} %copy-done.1, f32[32,64,512]{2,1,0:T(8,128)S(1)} %copy-done.2, f32[32,8,512]{2,1,0:T(8,128)S(1)} %get-tuple-element.16.eh, f32[32,8,512]{2,1,0:T(8,128)S(1)} %get-tuple-element.17.mh, f32[32,8,512]{2,1,0:T(8,128)S(1)} %get-tuple-element.18.rh), custom_call_target="tpu_custom_call" | custom-call | flops 73400320 | bytes 16777216 | tf_op jit(solution)/shard_map/inner/pallas_call | solution.py:336
  41.0 0.0 collective-permute-done.4.corner_even
  41.0 0.0 collective-permute-done.5.corner_odd
  41.0 0.0 collective-permute-done.2.got_even
  41.0 0.0 collective-permute-done.3.got_odd
  41.0 2.9 %outer.1 = f32[32,64,512]{2,1,0:T(8,128)} custom-call(f32[32,64,512]{2,1,0:T(8,128)S(1)} %copy-done, f32[32,64,512]{2,1,0:T(8,128)S(1)} %copy-done.1, f32[32,64,512]{2,1,0:T(8,128)S(1)} %copy-done.2, f32[32,8,512]{2,1,0:T(8,128)S(1)} %get-tuple-element.16.eh, f32[32,8,512]{2,1,0:T(8,128)S(1)} %get-tuple-element.17.mh, ...), custom_call_target="tpu_custom_call", output_to_operand_aliasing={{}: (10, {})} | custom-call | tf_op jit(solution)/shard_map/outer/pallas_call | solution.py:390
Async XLA Ops:
  0.0 2.2 %copy-start = (f32[32,64,512]{2,1,0:T(8,128)S(1)}, f32[32,64,512]{2,1,0:T(8,128)}, u32[]{:S(2)}) copy-start(f32[32,64,512]{2,1,0:T(8,128)} %e.5) | copy-start | bytes 12582916
  2.2 2.2 %copy-start.1 = (f32[32,64,512]{2,1,0:T(8,128)S(1)}, f32[32,64,512]{2,1,0:T(8,128)}, u32[]{:S(2)}) copy-start(f32[32,64,512]{2,1,0:T(8,128)} %m.5) | copy-start | bytes 12582916
  4.4 2.2 %copy-start.2 = (f32[32,64,512]{2,1,0:T(8,128)S(1)}, f32[32,64,512]{2,1,0:T(8,128)}, u32[]{:S(2)}) copy-start(f32[32,64,512]{2,1,0:T(8,128)} %r.5) | copy-start | bytes 12582916
  7.7 33.3 %collective-permute-start.2 = (f32[5,64,512]{2,1,0:T(8,128)S(1)}, f32[5,64,512]{2,1,0:T(8,128)S(1)}, u32[]{:S(2)}, u32[]{:S(2)}) collective-permute-start(f32[5,64,512]{2,1,0:T(8,128)S(1)} %get-tuple-element.19), channel_id=1, source_target_pairs={{0,8},{8,0},{16,24},{24,16},{32,40},{40,32},{48,56},{56,48},{64,72... | collective-permute-start | bytes 1966088 | tf_op jit(solution)/shard_map/ppermute | solution.py:185
  9.1 31.9 %collective-permute-start.3 = (f32[5,64,512]{2,1,0:T(8,128)S(1)}, f32[5,64,512]{2,1,0:T(8,128)S(1)}, u32[]{:S(2)}, u32[]{:S(2)}) collective-permute-start(f32[5,64,512]{2,1,0:T(8,128)S(1)} %get-tuple-element.20), channel_id=1, source_target_pairs={{8,16},{16,8},{24,32},{32,24},{40,48},{48,40},{56,64},{64,56},{72,... | collective-permute-start | bytes 1966088 | tf_op jit(solution)/shard_map/ppermute | solution.py:185
  12.7 4.3 %collective-permute-start = (f32[32,8,512]{2,1,0:T(8,128)S(1)}, f32[32,8,512]{2,1,0:T(8,128)S(1)}, u32[]{:S(2)}, u32[]{:S(2)}) collective-permute-start(f32[32,8,512]{2,1,0:T(8,128)S(1)} %get-tuple-element.14), channel_id=1, source_target_pairs={{0,1},{1,0},{2,3},{3,2},{4,5},{5,4},{6,7},{7,6},{8,9},{9,8},{10,11... | collective-permute-start | bytes 1572872 | tf_op jit(solution)/shard_map/ppermute | solution.py:185
  14.0 10.8 %collective-permute-start.1 = (f32[32,8,512]{2,1,0:T(8,128)S(1)}, f32[32,8,512]{2,1,0:T(8,128)S(1)}, u32[]{:S(2)}, u32[]{:S(2)}) collective-permute-start(f32[32,8,512]{2,1,0:T(8,128)S(1)} %get-tuple-element.15), channel_id=1, source_target_pairs={{1,2},{2,1},{3,4},{4,3},{5,6},{6,5},{9,10},{10,9},{11,12},{12,11},... | collective-permute-start | bytes 1572872 | tf_op jit(solution)/shard_map/ppermute | solution.py:185
  25.0 15.9 %collective-permute-start.4 = (f32[2,8,512]{2,1,0:T(8,128)S(1)}, f32[2,8,512]{2,1,0:T(8,128)S(1)}, u32[]{:S(2)}, u32[]{:S(2)}) collective-permute-start(f32[2,8,512]{2,1,0:T(8,128)S(1)} %get-tuple-element.21), channel_id=1, source_target_pairs={{0,8},{8,0},{16,24},{24,16},{32,40},{40,32},{48,56},{56,48},{64,72... | collective-permute-start | bytes 98312 | tf_op jit(solution)/shard_map/ppermute | solution.py:185
  25.7 15.3 %collective-permute-start.5 = (f32[2,8,512]{2,1,0:T(8,128)S(1)}, f32[2,8,512]{2,1,0:T(8,128)S(1)}, u32[]{:S(2)}, u32[]{:S(2)}) collective-permute-start(f32[2,8,512]{2,1,0:T(8,128)S(1)} %get-tuple-element.22), channel_id=1, source_target_pairs={{8,16},{16,8},{24,32},{32,24},{40,48},{48,40},{56,64},{64,56},{72,... | collective-permute-start | bytes 98312 | tf_op jit(solution)/shard_map/ppermute | solution.py:185

commit v2 on v0

v2 whole, which is shorter than its diff:
```python
import math

import jax
import jax.numpy as jnp
from jax import lax
from jax.experimental import pallas as pl
from jax.experimental.pallas import tpu as pltpu
from jax.sharding import PartitionSpec as P

sweep_weights = tuple((1.0 / (1.15 + 0.85 * math.cos(math.pi * (2 * j - 1) / 4.0)) for j in (1, 2)))

LANES = 128
ROWS = 8
VMEM = pl.BlockSpec(memory_space=pltpu.VMEM)
HBM = pl.BlockSpec(memory_space=pltpu.HBM)
F32 = jnp.float32


def lane_slices(nz):
    return [slice(k * LANES, (k + 1) * LANES) for k in range(nz // LANES)]


def iotas():
    row = lax.broadcasted_iota(jnp.int32, (ROWS, LANES), 0)
    lane = lax.broadcasted_iota(jnp.int32, (ROWS, LANES), 1)
    return row, lane


def next_lanes(vals, last_lane):
    turned = [pltpu.roll(v, LANES - 1, 1) for v in vals]
    return [jnp.where(last_lane, b, a) for a, b in zip(turned, turned[1:] + [0.0])]


def prev_lanes(vals, first_lane):
    turned = [pltpu.roll(v, 1, 1) for v in vals]
    return [jnp.where(first_lane, b, a) for a, b in zip(turned, [0.0] + turned[:-1])]


class Slab:
    def __init__(self, place, turning, ny, nz, row_ok):
        self.place, self.turning = place, turning
        self.strips = ny // ROWS
        self.tiles = lane_slices(nz)
        self.row_ok = row_ok
        _, lane = iotas()
        self.first_lane, self.last_lane = lane == 0, lane == LANES - 1

    def get(self, name, i, j):
        ref, at, row = self.place(name, i, j)
        return [ref[at, row : row + ROWS, s] for s in self.tiles]

    def put(self, name, i, j, vals):
        ref, at, row = self.place(name, i, j)
        for s, v in zip(self.tiles, vals):
            ref[at, row : row + ROWS, s] = v

    def load(self, i, strips, names):
        for j in strips:
            for name in names:
                ref, at = self.turning(name, i)
                vals = self.get(name, i, j)
                for row in (0, ROWS * (j + 1)) if j == self.strips else (ROWS * (j + 1),):
                    for k, v in enumerate(vals):
                        ref[at, k, row : row + ROWS, :] = v
            yield

    def shifted(self, name, i, j, by=0):
        ref, at = self.turning(name, i)
        if j == self.strips:
            row = {0: 0, 1: 1, -1: ROWS * (j + 1) - 1}[by]
        else:
            row = ROWS * (j + 1) + by
        return [ref[at, k, row : row + ROWS, :] for k in range(len(self.tiles))]

    def first(self, i, strips, keep=None):
        w = sweep_weights[0]
        n = self.strips
        strips = list(strips)

        def ahead(j):
            e, m = self.shifted("e", i, j), self.shifted("m", i, j)
            return (
                e,
                m,
                next_lanes(e, self.last_lane),
                prev_lanes(e, self.first_lane),
                next_lanes(m, self.last_lane),
                prev_lanes(m, self.first_lane),
            )

        here = ahead(strips[0])
        for j, after in zip(strips, strips[1:] + [None]):
            there = None if after is None else ahead(after)
            e, m, e_zp, e_zm, m_zp, m_zm = here
            e_up, e_dn = self.shifted("e", i, j, 1), self.shifted("e", i, j, -1)
            m_up, m_dn = self.shifted("m", i, j, 1), self.shifted("m", i, j, -1)
            e_xp, e_xm = self.get("e", i + 1, j), self.get("e", i - 1, j)
            m_xp, m_xm = self.get("m", i + 1, j), self.get("m", i - 1, j)
            r = self.get("r", i, j)
            made = []
            for k in range(len(self.tiles)):
                cx, cxm = m[k] + m_xp[k], m[k] + m_xm[k]
                cy, cy_dn = m[k] + m_up[k], m[k] + m_dn[k]
                cz, cz_dn = m[k] + m_zp[k], m[k] + m_zm[k]
                t = ((cx + cxm) + (cy + cy_dn)) + (cz + cz_dn)
                num = ((cx * e_xp[k] + cxm * e_xm[k]) + (cy * e_up[k] + cy_dn * e_dn[k])) + (
                    (cz * e_zp[k] + cz_dn * e_zm[k]) + (r[k] + r[k])
                )
                rt = 1.0 / t
                e1 = (1.0 - w) * e[k] + (w * rt) * num
                if j == n:
                    e1 = jnp.where(self.row_ok, e1, 0.0)
                if keep is not None:
                    e1 = jnp.where(keep, e1, 0.0)
                made.append((cx, cy, cz, rt, e1))
            cx, cy, cz, rt, e1 = zip(*made)
            self.put("cy", i, j, cy)
            self.put("e1", i, j, e1)
            if j < n:
                self.put("cx", i, j, cx)
                self.put("cz", i, j, cz)
                self.put("rt", i, j, rt)
            here = there
            yield

    def second(self, i, out, o):
        w = sweep_weights[1]

        def ahead(j):
            e, cz = self.shifted("e1", i, j), self.get("cz", i, j)
            return e, cz, next_lanes(e, self.last_lane), prev_lanes([a * b for a, b in zip(cz, e)], self.first_lane)

        here = ahead(0)
        for j in range(self.strips):
            there = ahead(j + 1) if j < self.strips - 1 else None
            e, cz, e_zp, h_dn = here
            e_up, e_dn = self.shifted("e1", i, j, 1), self.shifted("e1", i, j, -1)
            cy, cy_dn = self.shifted("cy", i, j), self.shifted("cy", i, j, -1)
            e_xp, e_xm = self.get("e1", i + 1, j), self.get("e1", i - 1, j)
            cx, cxm = self.get("cx", i, j), self.get("cx", i - 1, j)
            rt = self.get("rt", i, j)
            r = self.get("r", i, j)
            outs = []
            for k in range(len(self.tiles)):
                num = ((cx[k] * e_xp[k] + cxm[k] * e_xm[k]) + (cy[k] * e_up[k] + cy_dn[k] * e_dn[k])) + (
                    (cz[k] * e_zp[k] + h_dn[k]) + (r[k] + r[k])
                )
                outs.append((1.0 - w) * e[k] + (w * rt[k]) * num)
            for s, v in zip(self.tiles, outs):
                out[o, ROWS * j : ROWS * (j + 1), s] = v
            here = there
            yield


def run(*passes):
    passes = list(passes)
    while passes:
        passes = [p for p in passes if next(p, StopIteration) is not StopIteration]


RING1, RING2 = 6, 4
TURNED1, TURNED2 = ("e", "m"), ("e1", "cy")
MADE = ("e1", "cy", "cx", "cz", "rt")


def turned_shape(planes, ny, nz):
    return (planes, nz // LANES, ny + 2 * ROWS, LANES)


class Plane:
    def __init__(self, number, slot):
        self.number, self.slot = number, slot

    def __add__(self, by):
        return self.number + by

    def __sub__(self, by):
        return self.number - by


def number(i):
    return i.number if isinstance(i, Plane) else i


def ringed(first, last, size, ahead, body):
    @pl.loop(0, (last - first + 1) // size)
    def _(t):
        for k in range(size):
            i = first + size * t + k
            body(Plane(i, k), Plane(jnp.minimum(i + ahead, last), (k + ahead) % size))


def along_space(x, back):
    ns, nm = lax.axis_size("space"), lax.axis_size("member")
    hops = []
    for m in range(nm):
        step = 1 if m % 2 == 0 else -1
        for i in range(ns):
            to = (i + step, m) if 0 <= i + step < ns else (i, m + step)
            hops.append((i * nm + m, to[0] * nm + to[1]))
    return lax.ppermute(x, ("space", "member"), [(b, a) for a, b in hops] if back else hops)


def along_member(x, back):
    n = lax.axis_size("member")
    return lax.ppermute(x, "member", [((i + 1) % n, i) if back else (i, (i + 1) % n) for i in range(n)])


def sends_up(back):
    even = lax.rem(lax.axis_index("member"), 2) == 0
    return jnp.logical_not(even) if back else even


def has_next(axis):
    return lax.axis_index(axis) < lax.axis_size(axis) - 1


def has_prev(axis):
    return lax.axis_index(axis) > 0


def row_mask():
    row, _ = iotas()
    after, before = jnp.where(has_next("member"), 1, 0), jnp.where(has_prev("member"), 1, 0)
    return jnp.where(row < ROWS // 2, after, before) == 1


def send_kernel(e, m, r, to_next, to_prev, plane_out, plane_back, top, bottom, sems, plane_sems):
    nx, ny, nz = e.shape
    groups = nx // ROWS
    planes = []
    for dst, back in ((plane_out, False), (plane_back, True)):
        up = sends_up(back)
        two, one = jnp.where(up, nx - 2, 0), jnp.where(up, nx - 1, 0)
        for src, dst_at, size, at in ((e, 0, 2, two), (m, 2, 2, two), (r, 4, 1, one)):
            planes.append(
                pltpu.make_async_copy(src.at[pl.ds(at, size)], dst.at[dst_at : dst_at + size], plane_sems.at[len(planes)])
            )
    for c in planes:
        c.start()
    reads = []
    for k, src in enumerate((e, m, r)):
        for dst, at in ((top, 0), (bottom, ny - ROWS)):
            reads.append(pltpu.make_async_copy(src.at[:, at : at + ROWS], dst.at[k], sems.at[len(reads)]))
    for c in reads:
        c.start()
    for c in planes:
        c.wait()
    for dst, back in ((plane_out, False), (plane_back, True)):

        @pl.when(jnp.logical_not(jnp.where(sends_up(back), has_next("space"), has_prev("space"))))
        def _(dst=dst):
            dst[...] = jnp.zeros_like(dst)

    for c in reads:
        c.wait()
    next_ok, prev_ok = has_next("member"), has_prev("member")
    for n, (k, below, above) in enumerate(((0, 2, 0), (0, 1, 1), (1, 2, 0), (1, 1, 1), (2, 1, 0))):
        for g in range(groups):
            at = slice(ROWS * g, ROWS * (g + 1))
            to_next[groups * n + g] = jnp.where(next_ok, bottom[k, at, ROWS - below, :], 0.0)
            to_prev[groups * n + g] = jnp.where(prev_ok, top[k, at, above, :], 0.0)


def send(e, m, r):
    nx, ny, nz = e.shape
    rows = jax.ShapeDtypeStruct((5 * (nx // ROWS), ROWS, nz), F32)
    planes = jax.ShapeDtypeStruct((5, ny, nz), F32)
    strips = pltpu.VMEM((3, nx, ROWS, nz), F32)
    return pl.pallas_call(
        send_kernel,
        out_shape=[rows, rows, planes, planes],
        in_specs=[HBM] * 3,
        out_specs=[VMEM] * 4,
        scratch_shapes=[strips, strips, pltpu.SemaphoreType.DMA((6,)), pltpu.SemaphoreType.DMA((6,))],
        compiler_params=pltpu.CompilerParams(vmem_limit_bytes=8 * 2**20),
        name="send",
    )(e, m, r)


def halo_kernel(from_prev, from_next, _, eh, mh, rh, corner_out, corner_back):
    nx, _, nz = eh.shape
    groups = nx // ROWS
    for ref in (eh, mh, rh):
        ref[...] = jnp.zeros_like(ref)
    for n, (ref, below, above) in enumerate(((eh, 2, 0), (eh, 1, 1), (mh, 2, 0), (mh, 1, 1), (rh, 1, 0))):
        for g in range(groups):
            at = slice(ROWS * g, ROWS * (g + 1))
            ref[at, ROWS - below, :] = from_prev[groups * n + g]
            ref[at, above, :] = from_next[groups * n + g]
    for dst, back in ((corner_out, False), (corner_back, True)):
        up = sends_up(back)
        ok = jnp.where(up, has_next("space"), has_prev("space"))
        at = jnp.where(up, nx - 1, 0)
        dst[0] = jnp.where(ok, eh[at], 0.0)
        dst[1] = jnp.where(ok, mh[at], 0.0)


def halo(from_prev, from_next, nx, after):
    nz = from_prev.shape[2]
    strip = jax.ShapeDtypeStruct((nx, ROWS, nz), F32)
    corner = jax.ShapeDtypeStruct((2, ROWS, nz), F32)
    return pl.pallas_call(
        halo_kernel,
        out_shape=[strip] * 3 + [corner] * 2,
        in_specs=[VMEM] * 2 + [pl.BlockSpec(memory_space=pl.ANY)],
        out_specs=[VMEM] * 5,
        compiler_params=pltpu.CompilerParams(vmem_limit_bytes=2 * 2**20),
        name="halo",
    )(from_prev, from_next, after)


def middle_kernel(e, m, r, *rest):
    nx, ny, nz = e.shape
    arrays = dict(zip(("e", "m", "r") + MADE, (e, m, r) + rest))
    rings = dict(zip(TURNED1, rest[len(MADE) :]))
    slab = Slab(
        lambda name, i, j: (arrays[name], number(i), ROWS * j), lambda name, i: (rings[name], i.slot), ny, nz, None
    )
    strips = range(slab.strips)
    for k in range(RING1 // 2):
        run(slab.load(Plane(1 + k, k), strips, TURNED1))
    ringed(
        1,
        nx - 2,
        RING1,
        RING1 // 2,
        lambda i, later: run(slab.first(i, strips[1:-1]), slab.load(later, strips, TURNED1)),
    )


def middle(own):
    nx, ny, nz = own[0].shape
    return pl.pallas_call(
        middle_kernel,
        out_shape=[jax.ShapeDtypeStruct((nx, ny, nz), F32)] * len(MADE),
        in_specs=[VMEM] * 3,
        out_specs=[VMEM] * len(MADE),
        scratch_shapes=[pltpu.VMEM(turned_shape(RING1, ny, nz), F32)] * 2,
        compiler_params=pltpu.CompilerParams(vmem_limit_bytes=4 * 2**20),
        cost_estimate=pl.CostEstimate(flops=40 * nx * ny * nz, bytes_accessed=16 * nx * ny * nz, transcendentals=0),
        name="middle",
    )(*own)


def made_place(middles, ends, n, name, i, j):
    if 0 < j < n - 1:
        return middles[name], i, ROWS * j
    return ends[name], i, ROWS * {0: 0, n - 1: 1, n: 2}[j]


def inner_kernel(e, m, r, eh, mh, rh, *rest):
    nx, ny, nz = e.shape
    n = ny // ROWS
    own = {"e": (e, eh), "m": (m, mh), "r": (r, rh)}
    middles, rest = dict(zip(MADE, rest)), rest[len(MADE) :]
    out_hbm, ends, rest = rest[0], dict(zip(MADE, rest[1:])), rest[1 + len(MADE) :]
    rings, (out, sems) = dict(zip(TURNED1 + TURNED2, rest)), rest[4:]

    def place(name, i, j):
        if name in own:
            ref, strip = own[name]
            return (strip, number(i), 0) if j == n else (ref, number(i), ROWS * j)
        return made_place(middles, ends, n, name, number(i), j)

    slab = Slab(place, lambda name, i: (rings[name], i.slot), ny, nz, row_mask())

    def out_copy(i):
        return pltpu.make_async_copy(out.at[i], out_hbm.at[i], sems.at[i])

    around = [0, 1, n - 2, n - 1, n]
    for k in range(RING1 // 2):
        run(slab.load(Plane(1 + k, k), around, TURNED1))
    ringed(
        1,
        nx - 2,
        RING1,
        RING1 // 2,
        lambda i, later: run(slab.first(i, [0, n - 1, n]), slab.load(later, around, TURNED1)),
    )
    for k in range(RING2 // 2):
        run(slab.load(Plane(2 + k, k), range(n + 1), TURNED2))

    def step(i, later):
        run(slab.second(i, out, number(i)), slab.load(later, range(n + 1), TURNED2))
        out_copy(number(i)).start()

    ringed(2, nx - 3, RING2, RING2 // 2, step)

    @pl.loop(2, nx - 2)
    def _(i):
        out_copy(i).wait()


def inner(own, strips, middles):
    nx, ny, nz = own[0].shape
    args = (*own, *strips, *middles)
    return pl.pallas_call(
        inner_kernel,
        out_shape=[jax.ShapeDtypeStruct((nx, ny, nz), F32)] + [jax.ShapeDtypeStruct((nx, 3 * ROWS, nz), F32)] * len(MADE),
        in_specs=[VMEM] * len(args),
        out_specs=[HBM] + [VMEM] * len(MADE),
        scratch_shapes=[pltpu.VMEM(turned_shape(RING1, ny, nz), F32)] * 2
        + [pltpu.VMEM(turned_shape(RING2, ny, nz), F32)] * 2
        + [pltpu.VMEM((nx, ny, nz), F32), pltpu.SemaphoreType.DMA((nx,))],
        compiler_params=pltpu.CompilerParams(vmem_limit_bytes=9 * 2**20),
        cost_estimate=pl.CostEstimate(flops=40 * nx * ny * nz, bytes_accessed=16 * nx * ny * nz, transcendentals=0),
        name="inner",
    )(*args)


def outer_kernel(e, m, r, eh, mh, rh, got_out, got_back, corner_out, corner_back, *rest):
    nx, ny, nz = e.shape
    n = ny // ROWS
    count = len(MADE)
    middles, ends, rest = dict(zip(MADE, rest)), dict(zip(MADE, rest[count:])), rest[2 * count + 1 :]
    out_hbm, made, rest = rest[0], dict(zip(MADE, rest[1:])), rest[1 + count :]
    rings, (out, sems) = dict(zip(TURNED1 + TURNED2, rest)), rest[4:]
    own = {"e": e, "m": m, "r": r}
    strips = {"e": eh, "m": mh, "r": rh}
    got_at = {"e": 0, "m": 2}
    corner_at = {"e": 0, "m": 1}
    mask = row_mask()
    writes = []
    for side, (got, corner) in enumerate(((got_out, corner_out), (got_back, corner_back))):
        low = sends_up(side == 1)
        there = jnp.where(low, has_prev("space"), has_next("space"))

        def at(q, low=low):
            return jnp.where(low, q, nx - 1 - q)

        def place(name, q, j, got=got, corner=corner, low=low, at=at):
            if name in own:
                if q >= 0:
                    return (strips[name], at(q), 0) if j == n else (own[name], at(q), ROWS * j)
                if name == "r":
                    return got, 4, ROWS * j
                if j == n:
                    return corner, corner_at[name], 0
                return got, got_at[name] + jnp.where(low, 2 + q, -1 - q), ROWS * j
            if q <= 0:
                return made[name], 1 + q, ROWS * j
            i = jnp.where(low, q, nx - 2 - q) if name == "cx" else at(q)
            return made_place(middles, ends, n, name, i, j)

        slab = Slab(place, lambda name, q: (rings[name], q % 2), ny, nz, mask)
        keep = jnp.broadcast_to(jnp.where(there, 1, 0), (ROWS, LANES)) == 1
        run(slab.load(-1, range(n + 1), TURNED1), slab.load(0, range(n + 1), TURNED1))
        run(slab.load(1, range(n + 1), TURNED2))
        run(slab.first(-1, range(n), keep=keep))
        run(slab.first(0, range(n + 1)))
        run(slab.load(0, range(n + 1), TURNED2))
        for q in (0, 1):
            run(slab.second(q, out, 2 * side + q))
            c = pltpu.make_async_copy(out.at[2 * side + q], out_hbm.at[at(q)], sems.at[2 * side + q])
            c.start()
            writes.append(c)
    for c in writes:
        c.wait()


def outer(own, strips, got, corners, middles, ends, out):
    nx, ny, nz = own[0].shape
    args = (*own, *strips, *got, *corners, *middles, *ends)
    return pl.pallas_call(
        outer_kernel,
        out_shape=jax.ShapeDtypeStruct((nx, ny, nz), F32),
        in_specs=[VMEM] * len(args) + [HBM],
        out_specs=HBM,
        input_output_aliases={len(args): 0},
        scratch_shapes=[pltpu.VMEM((2, ny + ROWS, nz), F32)] * len(MADE)
        + [pltpu.VMEM(turned_shape(2, ny, nz), F32)] * 4
        + [pltpu.VMEM((4, ny, nz), F32), pltpu.SemaphoreType.DMA((4,))],
        compiler_params=pltpu.CompilerParams(vmem_limit_bytes=6 * 2**20),
        name="outer",
    )(*args, out)


def shards(residual, mobility, initial_guess):
    own = (initial_guess, mobility, residual)
    *rows, plane_out, plane_back = send(*(pltpu.with_memory_space_constraint(v, pltpu.HBM) for v in own))
    got = [along_space(v, back) for v, back in ((plane_out, False), (plane_back, True))]
    rows = [along_member(v, back) for v, back in zip(rows, (False, True))]
    middles = middle(own)
    *strips, corner_out, corner_back = halo(*rows, residual.shape[0], middles[-1])
    corners = [along_space(v, back) for v, back in ((corner_out, False), (corner_back, True))]
    out, *ends = inner(own, strips, middles)
    return outer(own, strips, got, corners, middles, ends, out)


def solution(mesh):
    placed = P("space", "member", None)
    return jax.shard_map(shards, mesh=mesh, in_specs=(placed,) * 3, out_specs=placed, check_vma=False)
```

time: 128 us -> 27.4 us (0.21)
  the two profiles are of different devices: /device:TPU:33 before, /device:TPU:64 now
where the time goes in v2:
time: 27.4 us; the launch traced here: 27.3 us
  Pallas kernels  14.9 us (54%)
  starting transfers between devices  11.4 us (42%)
  waiting for transfers between devices  0.94 us (3%)
    ppermute x4, starting transfers between devices, along_space(): lax.ppermute(x, ('space', 'member'), [(b, a) for a, b in hops] if back el...  8.4 us
    pallas_call x1, Pallas kernels, inner(): pl.pallas_call(inner_kernel, out_shape=[jax.ShapeDtypeStruct((nx, ny, nz)...  6.34 us
    pallas_call x1, Pallas kernels, middle(): pl.pallas_call(middle_kernel, out_shape=[jax.ShapeDtypeStruct((nx, ny, nz...  3.82 us
    ppermute x2, starting transfers between devices, along_member(): lax.ppermute(x, 'member', [((i + 1) % n, i) if back else (i, (i + 1) % n)...  2.96 us
    pallas_call x1, Pallas kernels, send(): pl.pallas_call(send_kernel, out_shape=[rows, rows, planes, planes], in_sp...  2.65 us
    pallas_call x1, Pallas kernels, outer(): pl.pallas_call(outer_kernel, out_shape=jax.ShapeDtypeStruct((nx, ny, nz),...  1.92 us
    ppermute x2, waiting for transfers between devices, along_member(): lax.ppermute(x, 'member', [((i + 1) % n, i) if back else (i, (i + 1) % n)...  0.93 us
  transfers between devices with their start and end apart: 6, of which 1 were waited for; matrix products, arithmetic and copies ran while one was open for 0% of the time, Pallas kernels for 38%

profile of v2, /device:TPU:64, one launch (start us, length us, event | category | flops | bytes accessed | tf_op | source)
XLA Modules:
  0.0 27.3 jit_solution(7168187486832873467)
XLA Ops:
  0.0 0.0 copy-start
  0.0 0.0 copy-start.1
  0.0 0.0 copy-start.2
  0.0 2.6 %send.1 = (f32[20,8,512]{2,1,0:T(8,128)S(1)}, f32[20,8,512]{2,1,0:T(8,128)S(1)}, f32[5,64,512]{2,1,0:T(8,128)S(1)}, f32[5,64,512]{2,1,0:T(8,128)S(1)}) custom-call(f32[32,64,512]{2,1,0:T(8,128)} %e.7, f32[32,64,512]{2,1,0:T(8,128)} %m.7, f32[32,64,512]{2,1,0:T(8,128)} %r.7), custom_call_target="tpu_custom_call" | custom-call | tf_op jit(solution)/shard_map/send/pallas_call | solution.py:270
  2.7 1.6 %collective-permute-start.2 = (f32[5,64,512]{2,1,0:T(8,128)S(1)}, f32[5,64,512]{2,1,0:T(8,128)S(1)}, u32[]{:S(2)}, u32[]{:S(2)}) collective-permute-start(f32[5,64,512]{2,1,0:T(8,128)S(1)} %get-tuple-element.31), channel_id=1, source_target_pairs={{0,8},{8,16},{16,24},{24,32},{32,40},{40,48},{48,56},{56,64},{64,7... | collective-permute-start | bytes 1966088 | tf_op jit(solution)/shard_map/ppermute | solution.py:201
  4.3 2.6 %collective-permute-start.3 = (f32[5,64,512]{2,1,0:T(8,128)S(1)}, f32[5,64,512]{2,1,0:T(8,128)S(1)}, u32[]{:S(2)}, u32[]{:S(2)}) collective-permute-start(f32[5,64,512]{2,1,0:T(8,128)S(1)} %get-tuple-element.32), channel_id=1, source_target_pairs={{8,0},{16,8},{24,16},{32,24},{40,32},{48,40},{56,48},{64,56},{72,6... | collective-permute-start | bytes 1966088 | tf_op jit(solution)/shard_map/ppermute | solution.py:201
  6.9 0.0 collective-permute-start
  6.9 3.0 %collective-permute-start.1 = (f32[20,8,512]{2,1,0:T(8,128)S(1)}, f32[20,8,512]{2,1,0:T(8,128)S(1)}, u32[]{:S(2)}, u32[]{:S(2)}) collective-permute-start(f32[20,8,512]{2,1,0:T(8,128)S(1)} %get-tuple-element.26), channel_id=1, source_target_pairs={{1,0},{2,1},{3,2},{4,3},{5,4},{6,5},{7,6},{0,7},{9,8},{10,9},{11,1... | collective-permute-start | bytes 983048 | tf_op jit(solution)/shard_map/ppermute | solution.py:206
  9.8 0.0 copy-done
  9.8 0.0 copy-done.1
  9.8 0.0 copy-done.2
  9.8 3.8 %middle.1 = (f32[32,64,512]{2,1,0:T(8,128)S(1)}, f32[32,64,512]{2,1,0:T(8,128)S(1)}, f32[32,64,512]{2,1,0:T(8,128)S(1)}, f32[32,64,512]{2,1,0:T(8,128)S(1)}, f32[32,64,512]{2,1,0:T(8,128)S(1)}) custom-call(f32[32,64,512]{2,1,0:T(8,128)S(1)} %copy-done, f32[32,64,512]{2,1,0:T(8,128)S(1)} %copy-done.1, f32[32,64,512]{2,1,0:T(8,128)S(1)} %copy-done.2), custom_call_target="tpu_custom_call" | custom-call | flops 41943040 | bytes 16777216 | tf_op jit(solution)/shard_map/middle/pallas_call | solution.py:334
  13.7 0.9 %collective-permute-done.from_prev = f32[20,8,512]{2,1,0:T(8,128)S(1)} collective-permute-done((f32[20,8,512]{2,1,0:T(8,128)S(1)}, f32[20,8,512]{2,1,0:T(8,128)S(1)}, u32[]{:S(2)}, u32[]{:S(2)}) %collective-permute-start) | collective-permute-done | bytes 327712 | tf_op jit(solution)/shard_map/ppermute | solution.py:206
  14.6 0.0 collective-permute-done.1.from_next
  14.6 0.2 halo.1
  14.8 0.1 collective-permute-start.4
  14.9 4.1 %collective-permute-start.5 = (f32[2,8,512]{2,1,0:T(8,128)S(1)}, f32[2,8,512]{2,1,0:T(8,128)S(1)}, u32[]{:S(2)}, u32[]{:S(2)}) collective-permute-start(f32[2,8,512]{2,1,0:T(8,128)S(1)} %get-tuple-element.34), channel_id=1, source_target_pairs={{8,0},{16,8},{24,16},{32,24},{40,32},{48,40},{56,48},{64,56},{72,6... | collective-permute-start | bytes 98312 | tf_op jit(solution)/shard_map/ppermute | solution.py:201
  19.0 6.3 %inner.1 = (f32[32,64,512]{2,1,0:T(8,128)}, f32[32,24,512]{2,1,0:T(8,128)S(1)}, f32[32,24,512]{2,1,0:T(8,128)S(1)}, f32[32,24,512]{2,1,0:T(8,128)S(1)}, f32[32,2...) custom-call(f32[32,64,512]{2,1,0:T(8,128)S(1)} %copy-done, f32[32,64,512]{2,1,0:T(8,128)S(1)} %copy-done.1, ...), custom_call_target="tpu_custom_call" | custom-call | flops 41943040 | bytes 16777216 | tf_op jit(solution)/shard_map/inner/pallas_call | solution.py:398
  25.4 0.0 collective-permute-done.4.corner_out
  25.4 0.0 collective-permute-done.5.corner_back
  25.4 0.0 collective-permute-done.2.got_out
  25.4 0.0 collective-permute-done.3.got_back
  25.4 1.9 %outer.1 = f32[32,64,512]{2,1,0:T(8,128)} custom-call(f32[32,64,512]{2,1,0:T(8,128)S(1)} %copy-done, f32[32,64,512]{2,1,0:T(8,128)S(1)} %copy-done.1, f32[32,64,512]{2,1,0:T(8,128)S(1)} %copy-done.2, f32[32,8,512]{2,1,0:T(8,128)S(1)} %get-tuple-element.28.eh, f32[32,8,512]{2,1,0:T(8,128)S(1)} %get-tuple-element.29.mh, ...), custom_call_target="tpu_custom_call", output_to_operand_aliasing={{}: (20, {})} | custom-call | tf_op jit(solution)/shard_map/outer/pallas_call | solution.py:465
Async XLA Ops:
  0.0 9.8 %copy-start = (f32[32,64,512]{2,1,0:T(8,128)S(1)}, f32[32,64,512]{2,1,0:T(8,128)}, u32[]{:S(2)}) copy-start(f32[32,64,512]{2,1,0:T(8,128)} %e.7) | copy-start | bytes 12582916
  0.0 9.8 %copy-start.1 = (f32[32,64,512]{2,1,0:T(8,128)S(1)}, f32[32,64,512]{2,1,0:T(8,128)}, u32[]{:S(2)}) copy-start(f32[32,64,512]{2,1,0:T(8,128)} %m.7) | copy-start | bytes 12582916
  0.0 9.8 %copy-start.2 = (f32[32,64,512]{2,1,0:T(8,128)S(1)}, f32[32,64,512]{2,1,0:T(8,128)}, u32[]{:S(2)}) copy-start(f32[32,64,512]{2,1,0:T(8,128)} %r.7) | copy-start | bytes 12582916
  2.7 22.7 %collective-permute-start.2 = (f32[5,64,512]{2,1,0:T(8,128)S(1)}, f32[5,64,512]{2,1,0:T(8,128)S(1)}, u32[]{:S(2)}, u32[]{:S(2)}) collective-permute-start(f32[5,64,512]{2,1,0:T(8,128)S(1)} %get-tuple-element.31), channel_id=1, source_target_pairs={{0,8},{8,16},{16,24},{24,32},{32,40},{40,48},{48,56},{56,64},{64,7... | collective-permute-start | bytes 1966088 | tf_op jit(solution)/shard_map/ppermute | solution.py:201
  4.3 21.1 %collective-permute-start.3 = (f32[5,64,512]{2,1,0:T(8,128)S(1)}, f32[5,64,512]{2,1,0:T(8,128)S(1)}, u32[]{:S(2)}, u32[]{:S(2)}) collective-permute-start(f32[5,64,512]{2,1,0:T(8,128)S(1)} %get-tuple-element.32), channel_id=1, source_target_pairs={{8,0},{16,8},{24,16},{32,24},{40,32},{48,40},{56,48},{64,56},{72,6... | collective-permute-start | bytes 1966088 | tf_op jit(solution)/shard_map/ppermute | solution.py:201
  6.9 7.7 %collective-permute-start = (f32[20,8,512]{2,1,0:T(8,128)S(1)}, f32[20,8,512]{2,1,0:T(8,128)S(1)}, u32[]{:S(2)}, u32[]{:S(2)}) collective-permute-start(f32[20,8,512]{2,1,0:T(8,128)S(1)} %get-tuple-element.25), channel_id=1, source_target_pairs={{0,1},{1,2},{2,3},{3,4},{4,5},{5,6},{6,7},{7,0},{8,9},{9,10},{10,1... | collective-permute-start | bytes 983048 | tf_op jit(solution)/shard_map/ppermute | solution.py:206
  6.9 7.7 %collective-permute-start.1 = (f32[20,8,512]{2,1,0:T(8,128)S(1)}, f32[20,8,512]{2,1,0:T(8,128)S(1)}, u32[]{:S(2)}, u32[]{:S(2)}) collective-permute-start(f32[20,8,512]{2,1,0:T(8,128)S(1)} %get-tuple-element.26), channel_id=1, source_target_pairs={{1,0},{2,1},{3,2},{4,3},{5,4},{6,5},{7,6},{0,7},{9,8},{10,9},{11,1... | collective-permute-start | bytes 983048 | tf_op jit(solution)/shard_map/ppermute | solution.py:206
  14.8 10.6 %collective-permute-start.4 = (f32[2,8,512]{2,1,0:T(8,128)S(1)}, f32[2,8,512]{2,1,0:T(8,128)S(1)}, u32[]{:S(2)}, u32[]{:S(2)}) collective-permute-start(f32[2,8,512]{2,1,0:T(8,128)S(1)} %get-tuple-element.33), channel_id=1, source_target_pairs={{0,8},{8,16},{16,24},{24,32},{32,40},{40,48},{48,56},{56,64},{64,7... | collective-permute-start | bytes 98312 | tf_op jit(solution)/shard_map/ppermute | solution.py:201
  14.9 10.5 %collective-permute-start.5 = (f32[2,8,512]{2,1,0:T(8,128)S(1)}, f32[2,8,512]{2,1,0:T(8,128)S(1)}, u32[]{:S(2)}, u32[]{:S(2)}) collective-permute-start(f32[2,8,512]{2,1,0:T(8,128)S(1)} %get-tuple-element.34), channel_id=1, source_target_pairs={{8,0},{16,8},{24,16},{32,24},{40,32},{48,40},{56,48},{64,56},{72,6... | collective-permute-start | bytes 98312 | tf_op jit(solution)/shard_map/ppermute | solution.py:201

commit v3 on v2

--- a/solution.py
+++ b/solution.py
@@ -72,7 +72,7 @@
             row = ROWS * (j + 1) + by
         return [ref[at, k, row : row + ROWS, :] for k in range(len(self.tiles))]
 
-    def first(self, i, strips, keep=None):
+    def first(self, i, strips, keep=None, e_before=True):
         w = sweep_weights[0]
         n = self.strips
         strips = list(strips)
@@ -94,7 +94,7 @@
             e, m, e_zp, e_zm, m_zp, m_zm = here
             e_up, e_dn = self.shifted("e", i, j, 1), self.shifted("e", i, j, -1)
             m_up, m_dn = self.shifted("m", i, j, 1), self.shifted("m", i, j, -1)
-            e_xp, e_xm = self.get("e", i + 1, j), self.get("e", i - 1, j)
+            e_xp, e_xm = self.get("e", i + 1, j), self.get("e", i - 1, j) if e_before else None
             m_xp, m_xm = self.get("m", i + 1, j), self.get("m", i - 1, j)
             r = self.get("r", i, j)
             made = []
@@ -103,9 +103,8 @@
                 cy, cy_dn = m[k] + m_up[k], m[k] + m_dn[k]
                 cz, cz_dn = m[k] + m_zp[k], m[k] + m_zm[k]
                 t = ((cx + cxm) + (cy + cy_dn)) + (cz + cz_dn)
-                num = ((cx * e_xp[k] + cxm * e_xm[k]) + (cy * e_up[k] + cy_dn * e_dn[k])) + (
-                    (cz * e_zp[k] + cz_dn * e_zm[k]) + (r[k] + r[k])
-                )
+                num_x = cx * e_xp[k] + cxm * e_xm[k] if e_before else cx * e_xp[k]
+                num = (num_x + (cy * e_up[k] + cy_dn * e_dn[k])) + ((cz * e_zp[k] + cz_dn * e_zm[k]) + (r[k] + r[k]))
                 rt = 1.0 / t
                 e1 = (1.0 - w) * e[k] + (w * rt) * num
                 if j == n:
@@ -158,7 +157,7 @@
         passes = [p for p in passes if next(p, StopIteration) is not StopIteration]
 
 
-RING1, RING2 = 6, 4
+RING = 6
 TURNED1, TURNED2 = ("e", "m"), ("e1", "cy")
 MADE = ("e1", "cy", "cx", "cz", "rt")
 
@@ -172,22 +171,17 @@
         self.number, self.slot = number, slot
 
     def __add__(self, by):
-        return self.number + by
+        return Plane(self.number + by, (self.slot + by) % RING)
 
     def __sub__(self, by):
-        return self.number - by
+        return self + -by
+
+    def load(self, by, last):
+        return Plane(jnp.minimum(self.number + by, last), (self.slot + by) % RING)
 
 
 def number(i):
     return i.number if isinstance(i, Plane) else i
-
-
-def ringed(first, last, size, ahead, body):
-    @pl.loop(0, (last - first + 1) // size)
-    def _(t):
-        for k in range(size):
-            i = first + size * t + k
-            body(Plane(i, k), Plane(jnp.minimum(i + ahead, last), (k + ahead) % size))
 
 
 def along_space(x, back):
@@ -225,54 +219,75 @@
     return jnp.where(row < ROWS // 2, after, before) == 1
 
 
-def send_kernel(e, m, r, to_next, to_prev, plane_out, plane_back, top, bottom, sems, plane_sems):
+def with_behind(e_behind, m_behind, m, r):
+    return r + (0.5 * e_behind) * (m + m_behind)
+
+
+def send_kernel(e, m, r, to_next, to_prev, plane_out, plane_back, top, bottom, planes, sems, plane_sems):
     nx, ny, nz = e.shape
     groups = nx // ROWS
-    planes = []
-    for dst, back in ((plane_out, False), (plane_back, True)):
-        up = sends_up(back)
-        two, one = jnp.where(up, nx - 2, 0), jnp.where(up, nx - 1, 0)
-        for src, dst_at, size, at in ((e, 0, 2, two), (m, 2, 2, two), (r, 4, 1, one)):
-            planes.append(
-                pltpu.make_async_copy(src.at[pl.ds(at, size)], dst.at[dst_at : dst_at + size], plane_sems.at[len(planes)])
-            )
-    for c in planes:
-        c.start()
     reads = []
     for k, src in enumerate((e, m, r)):
         for dst, at in ((top, 0), (bottom, ny - ROWS)):
-            reads.append(pltpu.make_async_copy(src.at[:, at : at + ROWS], dst.at[k], sems.at[len(reads)]))
+            rows = 1 if k == 2 else 2
+            first = 0 if at == 0 else ROWS - rows
+            here, there = src.at[:, at + first : at + first + rows], dst.at[k, :, first : first + rows]
+            reads.append(pltpu.make_async_copy(here, there, sems.at[len(reads)]))
     for c in reads:
         c.start()
-    for c in planes:
+    reads2 = []
+    for side, (dst, back) in enumerate(((plane_out, False), (plane_back, True))):
+        up = sends_up(back)
+        end, behind = jnp.where(up, nx - 1, 0), jnp.where(up, nx - 2, 1)
+        for src, at, to in (
+            (e, end, dst.at[0]),
+            (m, end, dst.at[1]),
+            (m, behind, dst.at[2]),
+            (e, behind, planes.at[2 * side]),
+            (r, end, planes.at[2 * side + 1]),
+        ):
+            reads2.append(pltpu.make_async_copy(src.at[at], to, plane_sems.at[len(reads2)]))
+    for c in reads2:
+        c.start()
+    for c in reads:
         c.wait()
-    for dst, back in ((plane_out, False), (plane_back, True)):
+    next_ok, prev_ok = has_next("member"), has_prev("member")
+    for dst, strips, end, behind, ok in (
+        (to_next, bottom, ROWS - 1, ROWS - 2, next_ok),
+        (to_prev, top, 0, 1, prev_ok),
+    ):
+        for g in range(groups):
+            at = slice(ROWS * g, ROWS * (g + 1))
+            e_behind, m_behind = strips[0, at, behind, :], strips[1, at, behind, :]
+            e_end, m_end, r_end = (strips[k, at, end, :] for k in range(3))
+            for n, v in enumerate((e_end, m_end, m_behind, with_behind(e_behind, m_behind, m_end, r_end))):
+                dst[groups * n + g] = jnp.where(ok, v, 0.0)
+    for c in reads2:
+        c.wait()
+    for side, (dst, back) in enumerate(((plane_out, False), (plane_back, True))):
+
+        @pl.loop(0, ny // ROWS)
+        def _(j, side=side, dst=dst):
+            at = pl.ds(pl.multiple_of(j * ROWS, ROWS), ROWS)
+            dst[3, at, :] = with_behind(planes[2 * side, at, :], dst[2, at, :], dst[1, at, :], planes[2 * side + 1, at, :])
 
         @pl.when(jnp.logical_not(jnp.where(sends_up(back), has_next("space"), has_prev("space"))))
         def _(dst=dst):
             dst[...] = jnp.zeros_like(dst)
 
-    for c in reads:
-        c.wait()
-    next_ok, prev_ok = has_next("member"), has_prev("member")
-    for n, (k, below, above) in enumerate(((0, 2, 0), (0, 1, 1), (1, 2, 0), (1, 1, 1), (2, 1, 0))):
-        for g in range(groups):
-            at = slice(ROWS * g, ROWS * (g + 1))
-            to_next[groups * n + g] = jnp.where(next_ok, bottom[k, at, ROWS - below, :], 0.0)
-            to_prev[groups * n + g] = jnp.where(prev_ok, top[k, at, above, :], 0.0)
-
 
 def send(e, m, r):
     nx, ny, nz = e.shape
-    rows = jax.ShapeDtypeStruct((5 * (nx // ROWS), ROWS, nz), F32)
-    planes = jax.ShapeDtypeStruct((5, ny, nz), F32)
+    rows = jax.ShapeDtypeStruct((4 * (nx // ROWS), ROWS, nz), F32)
+    planes = jax.ShapeDtypeStruct((4, ny, nz), F32)
     strips = pltpu.VMEM((3, nx, ROWS, nz), F32)
     return pl.pallas_call(
         send_kernel,
         out_shape=[rows, rows, planes, planes],
         in_specs=[HBM] * 3,
         out_specs=[VMEM] * 4,
-        scratch_shapes=[strips, strips, pltpu.SemaphoreType.DMA((6,)), pltpu.SemaphoreType.DMA((6,))],
+        scratch_shapes=[strips, strips, pltpu.VMEM((4, ny, nz), F32)]
+        + [pltpu.SemaphoreType.DMA((6,)), pltpu.SemaphoreType.DMA((10,))],
         compiler_params=pltpu.CompilerParams(vmem_limit_bytes=8 * 2**20),
         name="send",
     )(e, m, r)
@@ -283,7 +298,7 @@
     groups = nx // ROWS
     for ref in (eh, mh, rh):
         ref[...] = jnp.zeros_like(ref)
-    for n, (ref, below, above) in enumerate(((eh, 2, 0), (eh, 1, 1), (mh, 2, 0), (mh, 1, 1), (rh, 1, 0))):
+    for n, (ref, below, above) in enumerate(((eh, 1, 0), (mh, 1, 0), (mh, 2, 1), (rh, 1, 0))):
         for g in range(groups):
             at = slice(ROWS * g, ROWS * (g + 1))
             ref[at, ROWS - below, :] = from_prev[groups * n + g]
@@ -318,15 +333,14 @@
         lambda name, i, j: (arrays[name], number(i), ROWS * j), lambda name, i: (rings[name], i.slot), ny, nz, None
     )
     strips = range(slab.strips)
-    for k in range(RING1 // 2):
+    for k in range(RING // 2):
         run(slab.load(Plane(1 + k, k), strips, TURNED1))
-    ringed(
-        1,
-        nx - 2,
-        RING1,
-        RING1 // 2,
-        lambda i, later: run(slab.first(i, strips[1:-1]), slab.load(later, strips, TURNED1)),
-    )
+
+    @pl.loop(0, (nx - 2) // RING)
+    def _(t):
+        for k in range(RING):
+            i = Plane(1 + RING * t + k, k)
+            run(slab.first(i, strips[1:-1]), slab.load(i.load(RING // 2, nx - 2), strips, TURNED1))
 
 
 def middle(own):
@@ -336,56 +350,80 @@
         out_shape=[jax.ShapeDtypeStruct((nx, ny, nz), F32)] * len(MADE),
         in_specs=[VMEM] * 3,
         out_specs=[VMEM] * len(MADE),
-        scratch_shapes=[pltpu.VMEM(turned_shape(RING1, ny, nz), F32)] * 2,
+        scratch_shapes=[pltpu.VMEM(turned_shape(RING, ny, nz), F32)] * 2,
         compiler_params=pltpu.CompilerParams(vmem_limit_bytes=4 * 2**20),
         cost_estimate=pl.CostEstimate(flops=40 * nx * ny * nz, bytes_accessed=16 * nx * ny * nz, transcendentals=0),
         name="middle",
     )(*own)
 
 
-def made_place(middles, ends, n, name, i, j):
+def made_place(middles, ends, n, name, i, end, j):
     if 0 < j < n - 1:
         return middles[name], i, ROWS * j
-    return ends[name], i, ROWS * {0: 0, n - 1: 1, n: 2}[j]
+    return ends[name], end, ROWS * {0: 0, n - 1: 1, n: 2}[j]
 
 
 def inner_kernel(e, m, r, eh, mh, rh, *rest):
     nx, ny, nz = e.shape
     n = ny // ROWS
     own = {"e": (e, eh), "m": (m, mh), "r": (r, rh)}
-    middles, rest = dict(zip(MADE, rest)), rest[len(MADE) :]
-    out_hbm, ends, rest = rest[0], dict(zip(MADE, rest[1:])), rest[1 + len(MADE) :]
+    count = len(MADE)
+    middles, rest = dict(zip(MADE, rest)), rest[count:]
+    out_hbm, handed, rest = rest[0], dict(zip(MADE, rest[1:])), rest[1 + count :]
+    ends, rest = dict(zip(MADE, rest)), rest[count:]
     rings, (out, sems) = dict(zip(TURNED1 + TURNED2, rest)), rest[4:]
 
     def place(name, i, j):
         if name in own:
             ref, strip = own[name]
             return (strip, number(i), 0) if j == n else (ref, number(i), ROWS * j)
-        return made_place(middles, ends, n, name, number(i), j)
+        return made_place(middles, ends, n, name, number(i), i.slot, j)
 
     slab = Slab(place, lambda name, i: (rings[name], i.slot), ny, nz, row_mask())
+    around = [0, 1, n - 2, n - 1, n]
+    ahead, behind = RING // 2, 3
 
     def out_copy(i):
         return pltpu.make_async_copy(out.at[i], out_hbm.at[i], sems.at[i])
 
-    around = [0, 1, n - 2, n - 1, n]
-    for k in range(RING1 // 2):
+    def second(i):
+        return slab.second(i, out, number(i))
+
+    def first(i):
+        return [
+            slab.first(i, [0, n - 1, n]),
+            slab.load(i.load(ahead, nx - 2), around, TURNED1),
+            slab.load(i - 1, range(n + 1), TURNED2),
+        ]
+
+    def hand(k, slot):
+        for name in MADE:
+            handed[name][k] = ends[name][slot]
+
+    for k in range(ahead):
         run(slab.load(Plane(1 + k, k), around, TURNED1))
-    ringed(
-        1,
-        nx - 2,
-        RING1,
-        RING1 // 2,
-        lambda i, later: run(slab.first(i, [0, n - 1, n]), slab.load(later, around, TURNED1)),
-    )
-    for k in range(RING2 // 2):
-        run(slab.load(Plane(2 + k, k), range(n + 1), TURNED2))
-
-    def step(i, later):
-        run(slab.second(i, out, number(i)), slab.load(later, range(n + 1), TURNED2))
-        out_copy(number(i)).start()
-
-    ringed(2, nx - 3, RING2, RING2 // 2, step)
+    for k in range(RING):
+        i = Plane(1 + k, k)
+        if i.number < 2 + behind:
+            run(*first(i)[: 2 if k == 0 else 3])
+        else:
+            run(second(i - behind), *first(i))
+            out_copy(i.number - behind).start()
+    hand(0, 0)
+    hand(1, 1)
+
+    @pl.loop(1, (nx - 2) // RING)
+    def _(t):
+        for k in range(RING):
+            i = Plane(1 + RING * t + k, k)
+            run(second(i - behind), *first(i))
+            out_copy(i.number - behind).start()
+
+    hand(2, (nx - 4) % RING)
+    hand(3, (nx - 3) % RING)
+    for i in (nx - 4, nx - 3):
+        run(second(Plane(i, (i - 1) % RING)))
+        out_copy(i).start()
 
     @pl.loop(2, nx - 2)
     def _(i):
@@ -397,13 +435,13 @@
     args = (*own, *strips, *middles)
     return pl.pallas_call(
         inner_kernel,
-        out_shape=[jax.ShapeDtypeStruct((nx, ny, nz), F32)] + [jax.ShapeDtypeStruct((nx, 3 * ROWS, nz), F32)] * len(MADE),
+        out_shape=[jax.ShapeDtypeStruct((nx, ny, nz), F32)] + [jax.ShapeDtypeStruct((4, 3 * ROWS, nz), F32)] * len(MADE),
         in_specs=[VMEM] * len(args),
         out_specs=[HBM] + [VMEM] * len(MADE),
-        scratch_shapes=[pltpu.VMEM(turned_shape(RING1, ny, nz), F32)] * 2
-        + [pltpu.VMEM(turned_shape(RING2, ny, nz), F32)] * 2
+        scratch_shapes=[pltpu.VMEM((RING, 3 * ROWS, nz), F32)] * len(MADE)
+        + [pltpu.VMEM(turned_shape(RING, ny, nz), F32)] * 4
         + [pltpu.VMEM((nx, ny, nz), F32), pltpu.SemaphoreType.DMA((nx,))],
-        compiler_params=pltpu.CompilerParams(vmem_limit_bytes=9 * 2**20),
+        compiler_params=pltpu.CompilerParams(vmem_limit_bytes=11 * 2**20),
         cost_estimate=pl.CostEstimate(flops=40 * nx * ny * nz, bytes_accessed=16 * nx * ny * nz, transcendentals=0),
         name="inner",
     )(*args)
@@ -418,7 +456,7 @@
     rings, (out, sems) = dict(zip(TURNED1 + TURNED2, rest)), rest[4:]
     own = {"e": e, "m": m, "r": r}
     strips = {"e": eh, "m": mh, "r": rh}
-    got_at = {"e": 0, "m": 2}
+    got_at = {("e", -1): 0, ("m", -1): 1, ("m", -2): 2, ("r", -1): 3}
     corner_at = {"e": 0, "m": 1}
     mask = row_mask()
     writes = []
@@ -433,21 +471,20 @@
             if name in own:
                 if q >= 0:
                     return (strips[name], at(q), 0) if j == n else (own[name], at(q), ROWS * j)
-                if name == "r":
-                    return got, 4, ROWS * j
                 if j == n:
                     return corner, corner_at[name], 0
-                return got, got_at[name] + jnp.where(low, 2 + q, -1 - q), ROWS * j
+                return got, got_at[name, q], ROWS * j
             if q <= 0:
                 return made[name], 1 + q, ROWS * j
             i = jnp.where(low, q, nx - 2 - q) if name == "cx" else at(q)
-            return made_place(middles, ends, n, name, i, j)
+            end = jnp.where(low, q - 1, 3 - q if name == "cx" else 4 - q)
+            return made_place(middles, ends, n, name, i, end, j)
 
         slab = Slab(place, lambda name, q: (rings[name], q % 2), ny, nz, mask)
         keep = jnp.broadcast_to(jnp.where(there, 1, 0), (ROWS, LANES)) == 1
         run(slab.load(-1, range(n + 1), TURNED1), slab.load(0, range(n + 1), TURNED1))
         run(slab.load(1, range(n + 1), TURNED2))
-        run(slab.first(-1, range(n), keep=keep))
+        run(slab.first(-1, range(n), keep=keep, e_before=False))
         run(slab.first(0, range(n + 1)))
         run(slab.load(0, range(n + 1), TURNED2))
         for q in (0, 1):

time: 27.4 us -> 25.8 us (0.942)
  Pallas kernels: 14.9 us -> 14 us
  waiting for transfers between devices: 0.94 us -> 0.23 us
    ppermute x2, waiting for transfers between devices: 0.93 us -> 0.22 us  [along_member(): lax.ppermute(x, 'member', [((i + 1) % n, i) if back else (i, (i + 1) % n)...]
    pallas_call x1, Pallas kernels: 2.65 us -> 2.02 us  [send(): pl.pallas_call(send_kernel, out_shape=[rows, rows, planes, planes], in_sp...]
  transfers between devices with their start and end apart: 6 -> 6, of which waited for: 1 -> 1; matrix products, arithmetic and copies ran while one was open for 0% -> 0% of each run, Pallas kernels for 38% -> 39%
where the time goes in v3:
time: 25.8 us; the launch traced here: 25.7 us
  Pallas kernels  14 us (54%)
  starting transfers between devices  11.4 us (44%)
    ppermute x4, starting transfers between devices, along_space(): lax.ppermute(x, ('space', 'member'), [(b, a) for a, b in hops] if back el...  8.4 us
    pallas_call x1, Pallas kernels, inner(): pl.pallas_call(inner_kernel, out_shape=[jax.ShapeDtypeStruct((nx, ny, nz)...  6.12 us
    pallas_call x1, Pallas kernels, middle(): pl.pallas_call(middle_kernel, out_shape=[jax.ShapeDtypeStruct((nx, ny, nz...  3.82 us
    ppermute x2, starting transfers between devices, along_member(): lax.ppermute(x, 'member', [((i + 1) % n, i) if back else (i, (i + 1) % n)...  2.96 us
    pallas_call x1, Pallas kernels, send(): pl.pallas_call(send_kernel, out_shape=[rows, rows, planes, planes], in_sp...  2.02 us
    pallas_call x1, Pallas kernels, outer(): pl.pallas_call(outer_kernel, out_shape=jax.ShapeDtypeStruct((nx, ny, nz),...  1.89 us
  transfers between devices with their start and end apart: 6, of which 1 were waited for; matrix products, arithmetic and copies ran while one was open for 0% of the time, Pallas kernels for 39%

profile of v3, /device:TPU:64, one launch (start us, length us, event | category | flops | bytes accessed | tf_op | source)
XLA Modules:
  0.0 25.7 jit_solution(7899284901898665345)
XLA Ops:
  0.0 0.0 copy-start
  0.0 0.0 copy-start.1
  0.0 0.0 copy-start.2
  0.0 2.0 %send.1 = (f32[16,8,512]{2,1,0:T(8,128)S(1)}, f32[16,8,512]{2,1,0:T(8,128)S(1)}, f32[4,64,512]{2,1,0:T(8,128)S(1)}, f32[4,64,512]{2,1,0:T(8,128)S(1)}) custom-call(f32[32,64,512]{2,1,0:T(8,128)} %e.7, f32[32,64,512]{2,1,0:T(8,128)} %m.7, f32[32,64,512]{2,1,0:T(8,128)} %r.7), custom_call_target="tpu_custom_call" | custom-call | tf_op jit(solution)/shard_map/send/pallas_call | solution.py:284
  2.0 1.6 %collective-permute-start.2 = (f32[4,64,512]{2,1,0:T(8,128)S(1)}, f32[4,64,512]{2,1,0:T(8,128)S(1)}, u32[]{:S(2)}, u32[]{:S(2)}) collective-permute-start(f32[4,64,512]{2,1,0:T(8,128)S(1)} %get-tuple-element.31), channel_id=1, source_target_pairs={{0,8},{8,16},{16,24},{24,32},{32,40},{40,48},{48,56},{56,64},{64,7... | collective-permute-start | bytes 1572872 | tf_op jit(solution)/shard_map/ppermute | solution.py:195
  3.7 2.6 %collective-permute-start.3 = (f32[4,64,512]{2,1,0:T(8,128)S(1)}, f32[4,64,512]{2,1,0:T(8,128)S(1)}, u32[]{:S(2)}, u32[]{:S(2)}) collective-permute-start(f32[4,64,512]{2,1,0:T(8,128)S(1)} %get-tuple-element.32), channel_id=1, source_target_pairs={{8,0},{16,8},{24,16},{32,24},{40,32},{48,40},{56,48},{64,56},{72,6... | collective-permute-start | bytes 1572872 | tf_op jit(solution)/shard_map/ppermute | solution.py:195
  6.2 0.0 collective-permute-start
  6.2 3.0 %collective-permute-start.1 = (f32[16,8,512]{2,1,0:T(8,128)S(1)}, f32[16,8,512]{2,1,0:T(8,128)S(1)}, u32[]{:S(2)}, u32[]{:S(2)}) collective-permute-start(f32[16,8,512]{2,1,0:T(8,128)S(1)} %get-tuple-element.26), channel_id=1, source_target_pairs={{1,0},{2,1},{3,2},{4,3},{5,4},{6,5},{7,6},{0,7},{9,8},{10,9},{11,1... | collective-permute-start | bytes 786440 | tf_op jit(solution)/shard_map/ppermute | solution.py:200
  9.2 0.0 copy-done
  9.2 0.0 copy-done.1
  9.2 0.0 copy-done.2
  9.2 3.8 %middle.1 = (f32[32,64,512]{2,1,0:T(8,128)S(1)}, f32[32,64,512]{2,1,0:T(8,128)S(1)}, f32[32,64,512]{2,1,0:T(8,128)S(1)}, f32[32,64,512]{2,1,0:T(8,128)S(1)}, f32[32,64,512]{2,1,0:T(8,128)S(1)}) custom-call(f32[32,64,512]{2,1,0:T(8,128)S(1)} %copy-done, f32[32,64,512]{2,1,0:T(8,128)S(1)} %copy-done.1, f32[32,64,512]{2,1,0:T(8,128)S(1)} %copy-done.2), custom_call_target="tpu_custom_call" | custom-call | flops 41943040 | bytes 16777216 | tf_op jit(solution)/shard_map/middle/pallas_call | solution.py:348
  13.0 0.2 collective-permute-done.from_prev
  13.3 0.0 collective-permute-done.1.from_next
  13.3 0.2 halo.1
  13.5 0.1 collective-permute-start.4
  13.5 4.1 %collective-permute-start.5 = (f32[2,8,512]{2,1,0:T(8,128)S(1)}, f32[2,8,512]{2,1,0:T(8,128)S(1)}, u32[]{:S(2)}, u32[]{:S(2)}) collective-permute-start(f32[2,8,512]{2,1,0:T(8,128)S(1)} %get-tuple-element.34), channel_id=1, source_target_pairs={{8,0},{16,8},{24,16},{32,24},{40,32},{48,40},{56,48},{64,56},{72,6... | collective-permute-start | bytes 98312 | tf_op jit(solution)/shard_map/ppermute | solution.py:195
  17.7 6.1 %inner.1 = (f32[32,64,512]{2,1,0:T(8,128)}, f32[4,24,512]{2,1,0:T(8,128)S(1)}, f32[4,24,512]{2,1,0:T(8,128)S(1)}, f32[4,24,512]{2,1,0:T(8,128)S(1)}, f32[4,24,51...) custom-call(f32[32,64,512]{2,1,0:T(8,128)S(1)} %copy-done, f32[32,64,512]{2,1,0:T(8,128)S(1)} %copy-done.1, ...), custom_call_target="tpu_custom_call" | custom-call | flops 41943040 | bytes 16777216 | tf_op jit(solution)/shard_map/inner/pallas_call | solution.py:436
  23.8 0.0 collective-permute-done.4.corner_out
  23.8 0.0 collective-permute-done.5.corner_back
  23.8 0.0 collective-permute-done.2.got_out
  23.8 0.0 collective-permute-done.3.got_back
  23.8 1.9 %outer.1 = f32[32,64,512]{2,1,0:T(8,128)} custom-call(f32[32,64,512]{2,1,0:T(8,128)S(1)} %copy-done, f32[32,64,512]{2,1,0:T(8,128)S(1)} %copy-done.1, f32[32,64,512]{2,1,0:T(8,128)S(1)} %copy-done.2, f32[32,8,512]{2,1,0:T(8,128)S(1)} %get-tuple-element.28.eh, f32[32,8,512]{2,1,0:T(8,128)S(1)} %get-tuple-element.29.mh, ...), custom_call_target="tpu_custom_call", output_to_operand_aliasing={{}: (20, {})} | custom-call | tf_op jit(solution)/shard_map/outer/pallas_call | solution.py:502
Async XLA Ops:
  0.0 9.2 %copy-start = (f32[32,64,512]{2,1,0:T(8,128)S(1)}, f32[32,64,512]{2,1,0:T(8,128)}, u32[]{:S(2)}) copy-start(f32[32,64,512]{2,1,0:T(8,128)} %e.7) | copy-start | bytes 12582916
  0.0 9.2 %copy-start.1 = (f32[32,64,512]{2,1,0:T(8,128)S(1)}, f32[32,64,512]{2,1,0:T(8,128)}, u32[]{:S(2)}) copy-start(f32[32,64,512]{2,1,0:T(8,128)} %m.7) | copy-start | bytes 12582916
  0.0 9.2 %copy-start.2 = (f32[32,64,512]{2,1,0:T(8,128)S(1)}, f32[32,64,512]{2,1,0:T(8,128)}, u32[]{:S(2)}) copy-start(f32[32,64,512]{2,1,0:T(8,128)} %r.7) | copy-start | bytes 12582916
  2.0 21.8 %collective-permute-start.2 = (f32[4,64,512]{2,1,0:T(8,128)S(1)}, f32[4,64,512]{2,1,0:T(8,128)S(1)}, u32[]{:S(2)}, u32[]{:S(2)}) collective-permute-start(f32[4,64,512]{2,1,0:T(8,128)S(1)} %get-tuple-element.31), channel_id=1, source_target_pairs={{0,8},{8,16},{16,24},{24,32},{32,40},{40,48},{48,56},{56,64},{64,7... | collective-permute-start | bytes 1572872 | tf_op jit(solution)/shard_map/ppermute | solution.py:195
  3.7 20.1 %collective-permute-start.3 = (f32[4,64,512]{2,1,0:T(8,128)S(1)}, f32[4,64,512]{2,1,0:T(8,128)S(1)}, u32[]{:S(2)}, u32[]{:S(2)}) collective-permute-start(f32[4,64,512]{2,1,0:T(8,128)S(1)} %get-tuple-element.32), channel_id=1, source_target_pairs={{8,0},{16,8},{24,16},{32,24},{40,32},{48,40},{56,48},{64,56},{72,6... | collective-permute-start | bytes 1572872 | tf_op jit(solution)/shard_map/ppermute | solution.py:195
  6.2 7.0 %collective-permute-start = (f32[16,8,512]{2,1,0:T(8,128)S(1)}, f32[16,8,512]{2,1,0:T(8,128)S(1)}, u32[]{:S(2)}, u32[]{:S(2)}) collective-permute-start(f32[16,8,512]{2,1,0:T(8,128)S(1)} %get-tuple-element.25), channel_id=1, source_target_pairs={{0,1},{1,2},{2,3},{3,4},{4,5},{5,6},{6,7},{7,0},{8,9},{9,10},{10,1... | collective-permute-start | bytes 786440 | tf_op jit(solution)/shard_map/ppermute | solution.py:200
  6.2 7.0 %collective-permute-start.1 = (f32[16,8,512]{2,1,0:T(8,128)S(1)}, f32[16,8,512]{2,1,0:T(8,128)S(1)}, u32[]{:S(2)}, u32[]{:S(2)}) collective-permute-start(f32[16,8,512]{2,1,0:T(8,128)S(1)} %get-tuple-element.26), channel_id=1, source_target_pairs={{1,0},{2,1},{3,2},{4,3},{5,4},{6,5},{7,6},{0,7},{9,8},{10,9},{11,1... | collective-permute-start | bytes 786440 | tf_op jit(solution)/shard_map/ppermute | solution.py:200
  13.5 10.3 %collective-permute-start.4 = (f32[2,8,512]{2,1,0:T(8,128)S(1)}, f32[2,8,512]{2,1,0:T(8,128)S(1)}, u32[]{:S(2)}, u32[]{:S(2)}) collective-permute-start(f32[2,8,512]{2,1,0:T(8,128)S(1)} %get-tuple-element.33), channel_id=1, source_target_pairs={{0,8},{8,16},{16,24},{24,32},{32,40},{40,48},{48,56},{56,64},{64,7... | collective-permute-start | bytes 98312 | tf_op jit(solution)/shard_map/ppermute | solution.py:195
  13.5 10.3 %collective-permute-start.5 = (f32[2,8,512]{2,1,0:T(8,128)S(1)}, f32[2,8,512]{2,1,0:T(8,128)S(1)}, u32[]{:S(2)}, u32[]{:S(2)}) collective-permute-start(f32[2,8,512]{2,1,0:T(8,128)S(1)} %get-tuple-element.34), channel_id=1, source_target_pairs={{8,0},{16,8},{24,16},{32,24},{40,32},{48,40},{56,48},{64,56},{72,6... | collective-permute-start | bytes 98312 | tf_op jit(solution)/shard_map/ppermute | solution.py:195

commit v4 on v3

--- a/solution.py
+++ b/solution.py
@@ -369,9 +369,9 @@
     own = {"e": (e, eh), "m": (m, mh), "r": (r, rh)}
     count = len(MADE)
     middles, rest = dict(zip(MADE, rest)), rest[count:]
-    out_hbm, handed, rest = rest[0], dict(zip(MADE, rest[1:])), rest[1 + count :]
+    out_hbm, late, handed, rest = rest[0], rest[1], dict(zip(MADE, rest[2:])), rest[2 + count :]
     ends, rest = dict(zip(MADE, rest)), rest[count:]
-    rings, (out, sems) = dict(zip(TURNED1 + TURNED2, rest)), rest[4:]
+    rings, (out, sem) = dict(zip(TURNED1 + TURNED2, rest)), rest[4:]
 
     def place(name, i, j):
         if name in own:
@@ -384,7 +384,7 @@
     ahead, behind = RING // 2, 3
 
     def out_copy(i):
-        return pltpu.make_async_copy(out.at[i], out_hbm.at[i], sems.at[i])
+        return pltpu.make_async_copy(out.at[i], out_hbm.at[i], sem)
 
     def second(i):
         return slab.second(i, out, number(i))
@@ -421,13 +421,10 @@
 
     hand(2, (nx - 4) % RING)
     hand(3, (nx - 3) % RING)
-    for i in (nx - 4, nx - 3):
-        run(second(Plane(i, (i - 1) % RING)))
-        out_copy(i).start()
-
-    @pl.loop(2, nx - 2)
-    def _(i):
-        out_copy(i).wait()
+    for k, i in enumerate((nx - 4, nx - 3)):
+        run(slab.second(Plane(i, (i - 1) % RING), late, k))
+    sent = pl.ds(2, nx - 6)
+    pltpu.make_async_copy(out.at[sent], out_hbm.at[sent], sem).wait()
 
 
 def inner(own, strips, middles):
@@ -435,19 +432,20 @@
     args = (*own, *strips, *middles)
     return pl.pallas_call(
         inner_kernel,
-        out_shape=[jax.ShapeDtypeStruct((nx, ny, nz), F32)] + [jax.ShapeDtypeStruct((4, 3 * ROWS, nz), F32)] * len(MADE),
+        out_shape=[jax.ShapeDtypeStruct((nx, ny, nz), F32), jax.ShapeDtypeStruct((2, ny, nz), F32)]
+        + [jax.ShapeDtypeStruct((4, 3 * ROWS, nz), F32)] * len(MADE),
         in_specs=[VMEM] * len(args),
-        out_specs=[HBM] + [VMEM] * len(MADE),
+        out_specs=[HBM] + [VMEM] * (1 + len(MADE)),
         scratch_shapes=[pltpu.VMEM((RING, 3 * ROWS, nz), F32)] * len(MADE)
         + [pltpu.VMEM(turned_shape(RING, ny, nz), F32)] * 4
-        + [pltpu.VMEM((nx, ny, nz), F32), pltpu.SemaphoreType.DMA((nx,))],
+        + [pltpu.VMEM((nx, ny, nz), F32), pltpu.SemaphoreType.DMA],
         compiler_params=pltpu.CompilerParams(vmem_limit_bytes=11 * 2**20),
         cost_estimate=pl.CostEstimate(flops=40 * nx * ny * nz, bytes_accessed=16 * nx * ny * nz, transcendentals=0),
         name="inner",
     )(*args)
 
 
-def outer_kernel(e, m, r, eh, mh, rh, got_out, got_back, corner_out, corner_back, *rest):
+def outer_kernel(e, m, r, eh, mh, rh, got_out, got_back, corner_out, corner_back, late, *rest):
     nx, ny, nz = e.shape
     n = ny // ROWS
     count = len(MADE)
@@ -459,7 +457,8 @@
     got_at = {("e", -1): 0, ("m", -1): 1, ("m", -2): 2, ("r", -1): 3}
     corner_at = {"e": 0, "m": 1}
     mask = row_mask()
-    writes = []
+    writes = [pltpu.make_async_copy(late, out_hbm.at[nx - 4 : nx - 2], sems.at[4])]
+    writes[0].start()
     for side, (got, corner) in enumerate(((got_out, corner_out), (got_back, corner_back))):
         low = sends_up(side == 1)
         there = jnp.where(low, has_prev("space"), has_next("space"))
@@ -496,9 +495,9 @@
         c.wait()
 
 
-def outer(own, strips, got, corners, middles, ends, out):
+def outer(own, strips, got, corners, late, middles, ends, out):
     nx, ny, nz = own[0].shape
-    args = (*own, *strips, *got, *corners, *middles, *ends)
+    args = (*own, *strips, *got, *corners, late, *middles, *ends)
     return pl.pallas_call(
         outer_kernel,
         out_shape=jax.ShapeDtypeStruct((nx, ny, nz), F32),
@@ -507,7 +506,7 @@
         input_output_aliases={len(args): 0},
         scratch_shapes=[pltpu.VMEM((2, ny + ROWS, nz), F32)] * len(MADE)
         + [pltpu.VMEM(turned_shape(2, ny, nz), F32)] * 4
-        + [pltpu.VMEM((4, ny, nz), F32), pltpu.SemaphoreType.DMA((4,))],
+        + [pltpu.VMEM((4, ny, nz), F32), pltpu.SemaphoreType.DMA((5,))],
         compiler_params=pltpu.CompilerParams(vmem_limit_bytes=6 * 2**20),
         name="outer",
     )(*args, out)
@@ -521,8 +520,8 @@
     middles = middle(own)
     *strips, corner_out, corner_back = halo(*rows, residual.shape[0], middles[-1])
     corners = [along_space(v, back) for v, back in ((corner_out, False), (corner_back, True))]
-    out, *ends = inner(own, strips, middles)
-    return outer(own, strips, got, corners, middles, ends, out)
+    out, late, *ends = inner(own, strips, middles)
+    return outer(own, strips, got, corners, late, middles, ends, out)
 
 
 def solution(mesh):

time: 25.8 us -> 25.3 us (0.981)
  Pallas kernels: 14 us -> 13.5 us
    pallas_call x1, Pallas kernels: 6.12 us -> 5.58 us  [inner(): pl.pallas_call(inner_kernel, out_shape=[jax.ShapeDtypeStruct((nx, ny, nz)...]
  transfers between devices with their start and end apart: 6 -> 6, of which waited for: 1 -> 1; matrix products, arithmetic and copies ran while one was open for 0% -> 0% of each run, Pallas kernels for 39% -> 38%
where the time goes in v4:
time: 25.3 us; the launch traced here: 25.2 us
  Pallas kernels  13.5 us (53%)
  starting transfers between devices  11.4 us (45%)
    ppermute x4, starting transfers between devices, along_space(): lax.ppermute(x, ('space', 'member'), [(b, a) for a, b in hops] if back el...  8.4 us
    pallas_call x1, Pallas kernels, inner(): pl.pallas_call(inner_kernel, out_shape=[jax.ShapeDtypeStruct((nx, ny, nz)...  5.58 us
    pallas_call x1, Pallas kernels, middle(): pl.pallas_call(middle_kernel, out_shape=[jax.ShapeDtypeStruct((nx, ny, nz...  3.82 us
    ppermute x2, starting transfers between devices, along_member(): lax.ppermute(x, 'member', [((i + 1) % n, i) if back else (i, (i + 1) % n)...  2.96 us
    pallas_call x1, Pallas kernels, send(): pl.pallas_call(send_kernel, out_shape=[rows, rows, planes, planes], in_sp...  2.02 us
    pallas_call x1, Pallas kernels, outer(): pl.pallas_call(outer_kernel, out_shape=jax.ShapeDtypeStruct((nx, ny, nz),...  1.9 us
  transfers between devices with their start and end apart: 6, of which 1 were waited for; matrix products, arithmetic and copies ran while one was open for 0% of the time, Pallas kernels for 38%

profile of v4, /device:TPU:64, one launch (start us, length us, event | category | flops | bytes accessed | tf_op | source)
XLA Modules:
  0.0 25.2 jit_solution(4241433413968643931)
XLA Ops:
  0.0 0.0 copy-start
  0.0 0.0 copy-start.1
  0.0 0.0 copy-start.2
  0.0 2.0 %send.1 = (f32[16,8,512]{2,1,0:T(8,128)S(1)}, f32[16,8,512]{2,1,0:T(8,128)S(1)}, f32[4,64,512]{2,1,0:T(8,128)S(1)}, f32[4,64,512]{2,1,0:T(8,128)S(1)}) custom-call(f32[32,64,512]{2,1,0:T(8,128)} %e.7, f32[32,64,512]{2,1,0:T(8,128)} %m.7, f32[32,64,512]{2,1,0:T(8,128)} %r.7), custom_call_target="tpu_custom_call" | custom-call | tf_op jit(solution)/shard_map/send/pallas_call | solution.py:284
  2.0 1.6 %collective-permute-start.2 = (f32[4,64,512]{2,1,0:T(8,128)S(1)}, f32[4,64,512]{2,1,0:T(8,128)S(1)}, u32[]{:S(2)}, u32[]{:S(2)}) collective-permute-start(f32[4,64,512]{2,1,0:T(8,128)S(1)} %get-tuple-element.32), channel_id=1, source_target_pairs={{0,8},{8,16},{16,24},{24,32},{32,40},{40,48},{48,56},{56,64},{64,7... | collective-permute-start | bytes 1572872 | tf_op jit(solution)/shard_map/ppermute | solution.py:195
  3.7 2.6 %collective-permute-start.3 = (f32[4,64,512]{2,1,0:T(8,128)S(1)}, f32[4,64,512]{2,1,0:T(8,128)S(1)}, u32[]{:S(2)}, u32[]{:S(2)}) collective-permute-start(f32[4,64,512]{2,1,0:T(8,128)S(1)} %get-tuple-element.33), channel_id=1, source_target_pairs={{8,0},{16,8},{24,16},{32,24},{40,32},{48,40},{56,48},{64,56},{72,6... | collective-permute-start | bytes 1572872 | tf_op jit(solution)/shard_map/ppermute | solution.py:195
  6.2 0.0 collective-permute-start
  6.2 3.0 %collective-permute-start.1 = (f32[16,8,512]{2,1,0:T(8,128)S(1)}, f32[16,8,512]{2,1,0:T(8,128)S(1)}, u32[]{:S(2)}, u32[]{:S(2)}) collective-permute-start(f32[16,8,512]{2,1,0:T(8,128)S(1)} %get-tuple-element.27), channel_id=1, source_target_pairs={{1,0},{2,1},{3,2},{4,3},{5,4},{6,5},{7,6},{0,7},{9,8},{10,9},{11,1... | collective-permute-start | bytes 786440 | tf_op jit(solution)/shard_map/ppermute | solution.py:200
  9.2 0.0 copy-done
  9.2 0.0 copy-done.1
  9.2 0.0 copy-done.2
  9.2 3.8 %middle.1 = (f32[32,64,512]{2,1,0:T(8,128)S(1)}, f32[32,64,512]{2,1,0:T(8,128)S(1)}, f32[32,64,512]{2,1,0:T(8,128)S(1)}, f32[32,64,512]{2,1,0:T(8,128)S(1)}, f32[32,64,512]{2,1,0:T(8,128)S(1)}) custom-call(f32[32,64,512]{2,1,0:T(8,128)S(1)} %copy-done, f32[32,64,512]{2,1,0:T(8,128)S(1)} %copy-done.1, f32[32,64,512]{2,1,0:T(8,128)S(1)} %copy-done.2), custom_call_target="tpu_custom_call" | custom-call | flops 41943040 | bytes 16777216 | tf_op jit(solution)/shard_map/middle/pallas_call | solution.py:348
  13.0 0.2 collective-permute-done.from_prev
  13.3 0.0 collective-permute-done.1.from_next
  13.3 0.2 halo.1
  13.5 0.1 collective-permute-start.4
  13.5 4.1 %collective-permute-start.5 = (f32[2,8,512]{2,1,0:T(8,128)S(1)}, f32[2,8,512]{2,1,0:T(8,128)S(1)}, u32[]{:S(2)}, u32[]{:S(2)}) collective-permute-start(f32[2,8,512]{2,1,0:T(8,128)S(1)} %get-tuple-element.35), channel_id=1, source_target_pairs={{8,0},{16,8},{24,16},{32,24},{40,32},{48,40},{56,48},{64,56},{72,6... | collective-permute-start | bytes 98312 | tf_op jit(solution)/shard_map/ppermute | solution.py:195
  17.7 5.6 %inner.1 = (f32[32,64,512]{2,1,0:T(8,128)}, f32[2,64,512]{2,1,0:T(8,128)S(1)}, f32[4,24,512]{2,1,0:T(8,128)S(1)}, f32[4,24,512]{2,1,0:T(8,128)S(1)}, f32[4,24,51...) custom-call(f32[32,64,512]{2,1,0:T(8,128)S(1)} %copy-done, f32[32,64,512]{2,1,0:T(8,128)S(1)} %copy-done.1, ...), custom_call_target="tpu_custom_call" | custom-call | flops 41943040 | bytes 16777216 | tf_op jit(solution)/shard_map/inner/pallas_call | solution.py:433
  23.3 0.0 collective-permute-done.4.corner_out
  23.3 0.0 collective-permute-done.5.corner_back
  23.3 0.0 collective-permute-done.2.got_out
  23.3 0.0 collective-permute-done.3.got_back
  23.3 1.9 %outer.1 = f32[32,64,512]{2,1,0:T(8,128)} custom-call(f32[32,64,512]{2,1,0:T(8,128)S(1)} %copy-done, f32[32,64,512]{2,1,0:T(8,128)S(1)} %copy-done.1, f32[32,64,512]{2,1,0:T(8,128)S(1)} %copy-done.2, f32[32,8,512]{2,1,0:T(8,128)S(1)} %get-tuple-element.29.eh, f32[32,8,512]{2,1,0:T(8,128)S(1)} %get-tuple-element.30.mh, ...), custom_call_target="tpu_custom_call", output_to_operand_aliasing={{}: (21, {})} | custom-call | tf_op jit(solution)/shard_map/outer/pallas_call | solution.py:501
Async XLA Ops:
  0.0 9.2 %copy-start = (f32[32,64,512]{2,1,0:T(8,128)S(1)}, f32[32,64,512]{2,1,0:T(8,128)}, u32[]{:S(2)}) copy-start(f32[32,64,512]{2,1,0:T(8,128)} %e.7) | copy-start | bytes 12582916
  0.0 9.2 %copy-start.1 = (f32[32,64,512]{2,1,0:T(8,128)S(1)}, f32[32,64,512]{2,1,0:T(8,128)}, u32[]{:S(2)}) copy-start(f32[32,64,512]{2,1,0:T(8,128)} %m.7) | copy-start | bytes 12582916
  0.0 9.2 %copy-start.2 = (f32[32,64,512]{2,1,0:T(8,128)S(1)}, f32[32,64,512]{2,1,0:T(8,128)}, u32[]{:S(2)}) copy-start(f32[32,64,512]{2,1,0:T(8,128)} %r.7) | copy-start | bytes 12582916
  2.0 21.2 %collective-permute-start.2 = (f32[4,64,512]{2,1,0:T(8,128)S(1)}, f32[4,64,512]{2,1,0:T(8,128)S(1)}, u32[]{:S(2)}, u32[]{:S(2)}) collective-permute-start(f32[4,64,512]{2,1,0:T(8,128)S(1)} %get-tuple-element.32), channel_id=1, source_target_pairs={{0,8},{8,16},{16,24},{24,32},{32,40},{40,48},{48,56},{56,64},{64,7... | collective-permute-start | bytes 1572872 | tf_op jit(solution)/shard_map/ppermute | solution.py:195
  3.7 19.6 %collective-permute-start.3 = (f32[4,64,512]{2,1,0:T(8,128)S(1)}, f32[4,64,512]{2,1,0:T(8,128)S(1)}, u32[]{:S(2)}, u32[]{:S(2)}) collective-permute-start(f32[4,64,512]{2,1,0:T(8,128)S(1)} %get-tuple-element.33), channel_id=1, source_target_pairs={{8,0},{16,8},{24,16},{32,24},{40,32},{48,40},{56,48},{64,56},{72,6... | collective-permute-start | bytes 1572872 | tf_op jit(solution)/shard_map/ppermute | solution.py:195
  6.2 7.0 %collective-permute-start = (f32[16,8,512]{2,1,0:T(8,128)S(1)}, f32[16,8,512]{2,1,0:T(8,128)S(1)}, u32[]{:S(2)}, u32[]{:S(2)}) collective-permute-start(f32[16,8,512]{2,1,0:T(8,128)S(1)} %get-tuple-element.26), channel_id=1, source_target_pairs={{0,1},{1,2},{2,3},{3,4},{4,5},{5,6},{6,7},{7,0},{8,9},{9,10},{10,1... | collective-permute-start | bytes 786440 | tf_op jit(solution)/shard_map/ppermute | solution.py:200
  6.2 7.0 %collective-permute-start.1 = (f32[16,8,512]{2,1,0:T(8,128)S(1)}, f32[16,8,512]{2,1,0:T(8,128)S(1)}, u32[]{:S(2)}, u32[]{:S(2)}) collective-permute-start(f32[16,8,512]{2,1,0:T(8,128)S(1)} %get-tuple-element.27), channel_id=1, source_target_pairs={{1,0},{2,1},{3,2},{4,3},{5,4},{6,5},{7,6},{0,7},{9,8},{10,9},{11,1... | collective-permute-start | bytes 786440 | tf_op jit(solution)/shard_map/ppermute | solution.py:200
  13.5 9.8 %collective-permute-start.4 = (f32[2,8,512]{2,1,0:T(8,128)S(1)}, f32[2,8,512]{2,1,0:T(8,128)S(1)}, u32[]{:S(2)}, u32[]{:S(2)}) collective-permute-start(f32[2,8,512]{2,1,0:T(8,128)S(1)} %get-tuple-element.34), channel_id=1, source_target_pairs={{0,8},{8,16},{16,24},{24,32},{32,40},{40,48},{48,56},{56,64},{64,7... | collective-permute-start | bytes 98312 | tf_op jit(solution)/shard_map/ppermute | solution.py:195
  13.5 9.7 %collective-permute-start.5 = (f32[2,8,512]{2,1,0:T(8,128)S(1)}, f32[2,8,512]{2,1,0:T(8,128)S(1)}, u32[]{:S(2)}, u32[]{:S(2)}) collective-permute-start(f32[2,8,512]{2,1,0:T(8,128)S(1)} %get-tuple-element.35), channel_id=1, source_target_pairs={{8,0},{16,8},{24,16},{32,24},{40,32},{48,40},{56,48},{64,56},{72,6... | collective-permute-start | bytes 98312 | tf_op jit(solution)/shard_map/ppermute | solution.py:195

commit v5 on v4

--- a/solution.py
+++ b/solution.py
@@ -158,6 +158,7 @@
 
 
 RING = 6
+MIDDLE_RING = 10
 TURNED1, TURNED2 = ("e", "m"), ("e1", "cy")
 MADE = ("e1", "cy", "cx", "cz", "rt")
 
@@ -167,17 +168,17 @@
 
 
 class Plane:
-    def __init__(self, number, slot):
-        self.number, self.slot = number, slot
+    def __init__(self, number, slot, ring=RING):
+        self.number, self.slot, self.ring = number, slot % ring, ring
 
     def __add__(self, by):
-        return Plane(self.number + by, (self.slot + by) % RING)
+        return Plane(self.number + by, self.slot + by, self.ring)
 
     def __sub__(self, by):
         return self + -by
 
     def load(self, by, last):
-        return Plane(jnp.minimum(self.number + by, last), (self.slot + by) % RING)
+        return Plane(jnp.minimum(self.number + by, last), self.slot + by, self.ring)
 
 
 def number(i):
@@ -333,14 +334,14 @@
         lambda name, i, j: (arrays[name], number(i), ROWS * j), lambda name, i: (rings[name], i.slot), ny, nz, None
     )
     strips = range(slab.strips)
-    for k in range(RING // 2):
-        run(slab.load(Plane(1 + k, k), strips, TURNED1))
-
-    @pl.loop(0, (nx - 2) // RING)
+    for k in range(3):
+        run(slab.load(Plane(1 + k, k, MIDDLE_RING), strips, TURNED1))
+
+    @pl.loop(0, (nx - 2) // MIDDLE_RING)
     def _(t):
-        for k in range(RING):
-            i = Plane(1 + RING * t + k, k)
-            run(slab.first(i, strips[1:-1]), slab.load(i.load(RING // 2, nx - 2), strips, TURNED1))
+        for k in range(MIDDLE_RING):
+            i = Plane(1 + MIDDLE_RING * t + k, k, MIDDLE_RING)
+            run(slab.first(i, strips[1:-1]), slab.load(i.load(3, nx - 2), strips, TURNED1))
 
 
 def middle(own):
@@ -350,8 +351,8 @@
         out_shape=[jax.ShapeDtypeStruct((nx, ny, nz), F32)] * len(MADE),
         in_specs=[VMEM] * 3,
         out_specs=[VMEM] * len(MADE),
-        scratch_shapes=[pltpu.VMEM(turned_shape(RING, ny, nz), F32)] * 2,
-        compiler_params=pltpu.CompilerParams(vmem_limit_bytes=4 * 2**20),
+        scratch_shapes=[pltpu.VMEM(turned_shape(MIDDLE_RING, ny, nz), F32)] * 2,
+        compiler_params=pltpu.CompilerParams(vmem_limit_bytes=5 * 2**20),
         cost_estimate=pl.CostEstimate(flops=40 * nx * ny * nz, bytes_accessed=16 * nx * ny * nz, transcendentals=0),
         name="middle",
     )(*own)
@@ -369,9 +370,9 @@
     own = {"e": (e, eh), "m": (m, mh), "r": (r, rh)}
     count = len(MADE)
     middles, rest = dict(zip(MADE, rest)), rest[count:]
-    out_hbm, late, handed, rest = rest[0], rest[1], dict(zip(MADE, rest[2:])), rest[2 + count :]
+    out_hbm, out, handed, rest = rest[0], rest[1], dict(zip(MADE, rest[2:])), rest[2 + count :]
     ends, rest = dict(zip(MADE, rest)), rest[count:]
-    rings, (out, sem) = dict(zip(TURNED1 + TURNED2, rest)), rest[4:]
+    rings, (sem,) = dict(zip(TURNED1 + TURNED2, rest)), rest[4:]
 
     def place(name, i, j):
         if name in own:
@@ -383,8 +384,9 @@
     around = [0, 1, n - 2, n - 1, n]
     ahead, behind = RING // 2, 3
 
-    def out_copy(i):
-        return pltpu.make_async_copy(out.at[i], out_hbm.at[i], sem)
+    def send_out(first, count):
+        at = pl.ds(first, count)
+        return pltpu.make_async_copy(out.at[at], out_hbm.at[at], sem)
 
     def second(i):
         return slab.second(i, out, number(i))
@@ -408,23 +410,29 @@
             run(*first(i)[: 2 if k == 0 else 3])
         else:
             run(second(i - behind), *first(i))
-            out_copy(i.number - behind).start()
     hand(0, 0)
     hand(1, 1)
+    send_out(2, 2).start()
 
     @pl.loop(1, (nx - 2) // RING)
     def _(t):
+        @pl.when(t > 1)
+        def _():
+            send_out(4 + RING * (t - 2), RING).start()
+
         for k in range(RING):
             i = Plane(1 + RING * t + k, k)
             run(second(i - behind), *first(i))
-            out_copy(i.number - behind).start()
 
     hand(2, (nx - 4) % RING)
     hand(3, (nx - 3) % RING)
-    for k, i in enumerate((nx - 4, nx - 3)):
-        run(slab.second(Plane(i, (i - 1) % RING), late, k))
-    sent = pl.ds(2, nx - 6)
-    pltpu.make_async_copy(out.at[sent], out_hbm.at[sent], sem).wait()
+    for i in (nx - 4, nx - 3):
+        run(second(Plane(i, i - 1)))
+    send_out(2, unsent(nx) - 2).wait()
+
+
+def unsent(nx):
+    return max(4, nx - 4 - RING)
 
 
 def inner(own, strips, middles):
@@ -432,20 +440,20 @@
     args = (*own, *strips, *middles)
     return pl.pallas_call(
         inner_kernel,
-        out_shape=[jax.ShapeDtypeStruct((nx, ny, nz), F32), jax.ShapeDtypeStruct((2, ny, nz), F32)]
+        out_shape=[jax.ShapeDtypeStruct((nx, ny, nz), F32)] * 2
         + [jax.ShapeDtypeStruct((4, 3 * ROWS, nz), F32)] * len(MADE),
         in_specs=[VMEM] * len(args),
         out_specs=[HBM] + [VMEM] * (1 + len(MADE)),
         scratch_shapes=[pltpu.VMEM((RING, 3 * ROWS, nz), F32)] * len(MADE)
         + [pltpu.VMEM(turned_shape(RING, ny, nz), F32)] * 4
-        + [pltpu.VMEM((nx, ny, nz), F32), pltpu.SemaphoreType.DMA],
-        compiler_params=pltpu.CompilerParams(vmem_limit_bytes=11 * 2**20),
+        + [pltpu.SemaphoreType.DMA],
+        compiler_params=pltpu.CompilerParams(vmem_limit_bytes=7 * 2**20),
         cost_estimate=pl.CostEstimate(flops=40 * nx * ny * nz, bytes_accessed=16 * nx * ny * nz, transcendentals=0),
         name="inner",
     )(*args)
 
 
-def outer_kernel(e, m, r, eh, mh, rh, got_out, got_back, corner_out, corner_back, late, *rest):
+def outer_kernel(e, m, r, eh, mh, rh, got_out, got_back, corner_out, corner_back, second, *rest):
     nx, ny, nz = e.shape
     n = ny // ROWS
     count = len(MADE)
@@ -457,7 +465,8 @@
     got_at = {("e", -1): 0, ("m", -1): 1, ("m", -2): 2, ("r", -1): 3}
     corner_at = {"e": 0, "m": 1}
     mask = row_mask()
-    writes = [pltpu.make_async_copy(late, out_hbm.at[nx - 4 : nx - 2], sems.at[4])]
+    late = pl.ds(unsent(nx), nx - 2 - unsent(nx))
+    writes = [pltpu.make_async_copy(second.at[late], out_hbm.at[late], sems.at[4])]
     writes[0].start()
     for side, (got, corner) in enumerate(((got_out, corner_out), (got_back, corner_back))):
         low = sends_up(side == 1)
@@ -495,9 +504,9 @@
         c.wait()
 
 
-def outer(own, strips, got, corners, late, middles, ends, out):
+def outer(own, strips, got, corners, second, middles, ends, out):
     nx, ny, nz = own[0].shape
-    args = (*own, *strips, *got, *corners, late, *middles, *ends)
+    args = (*own, *strips, *got, *corners, second, *middles, *ends)
     return pl.pallas_call(
         outer_kernel,
         out_shape=jax.ShapeDtypeStruct((nx, ny, nz), F32),
@@ -520,8 +529,8 @@
     middles = middle(own)
     *strips, corner_out, corner_back = halo(*rows, residual.shape[0], middles[-1])
     corners = [along_space(v, back) for v, back in ((corner_out, False), (corner_back, True))]
-    out, late, *ends = inner(own, strips, middles)
-    return outer(own, strips, got, corners, late, middles, ends, out)
+    out, second, *ends = inner(own, strips, middles)
+    return outer(own, strips, got, corners, second, middles, ends, out)
 
 
 def solution(mesh):

time: 25.3 us -> 24.8 us (0.980)
  Pallas kernels: 13.5 us -> 12.9 us
    pallas_call x1, Pallas kernels: 5.58 us -> 5.13 us  [inner(): pl.pallas_call(inner_kernel, out_shape=[jax.ShapeDtypeStruct((nx, ny, nz)...]
  transfers between devices with their start and end apart: 6 -> 6, of which waited for: 1 -> 1; matrix products, arithmetic and copies ran while one was open for 0% -> 0% of each run, Pallas kernels for 38% -> 36%
where the time goes in v5:
time: 24.8 us
  Pallas kernels  12.9 us (52%)
  starting transfers between devices  11.4 us (46%)
  waiting for transfers between devices  0.4 us (2%)
    ppermute x4, starting transfers between devices, along_space(): lax.ppermute(x, ('space', 'member'), [(b, a) for a, b in hops] if back el...  8.4 us
    pallas_call x1, Pallas kernels, inner(): pl.pallas_call(inner_kernel, out_shape=[jax.ShapeDtypeStruct((nx, ny, nz)...  5.13 us
    pallas_call x1, Pallas kernels, middle(): pl.pallas_call(middle_kernel, out_shape=[jax.ShapeDtypeStruct((nx, ny, nz...  3.65 us
    ppermute x2, starting transfers between devices, along_member(): lax.ppermute(x, 'member', [((i + 1) % n, i) if back else (i, (i + 1) % n)...  2.96 us
    pallas_call x1, Pallas kernels, send(): pl.pallas_call(send_kernel, out_shape=[rows, rows, planes, planes], in_sp...  2.02 us
    pallas_call x1, Pallas kernels, outer(): pl.pallas_call(outer_kernel, out_shape=jax.ShapeDtypeStruct((nx, ny, nz),...  1.91 us
  transfers between devices with their start and end apart: 6, of which 1 were waited for; matrix products, arithmetic and copies ran while one was open for 0% of the time, Pallas kernels for 36%

profile of v5, /device:TPU:64, one launch (start us, length us, event | category | flops | bytes accessed | tf_op | source)
XLA Modules:
  0.0 24.8 jit_solution(18089874539509519588)
XLA Ops:
  0.0 0.0 copy-start
  0.0 0.0 copy-start.1
  0.0 0.0 copy-start.2
  0.0 2.0 %send.1 = (f32[16,8,512]{2,1,0:T(8,128)S(1)}, f32[16,8,512]{2,1,0:T(8,128)S(1)}, f32[4,64,512]{2,1,0:T(8,128)S(1)}, f32[4,64,512]{2,1,0:T(8,128)S(1)}) custom-call(f32[32,64,512]{2,1,0:T(8,128)} %e.7, f32[32,64,512]{2,1,0:T(8,128)} %m.7, f32[32,64,512]{2,1,0:T(8,128)} %r.7), custom_call_target="tpu_custom_call" | custom-call | tf_op jit(solution)/shard_map/send/pallas_call | solution.py:285
  2.0 1.6 %collective-permute-start.2 = (f32[4,64,512]{2,1,0:T(8,128)S(1)}, f32[4,64,512]{2,1,0:T(8,128)S(1)}, u32[]{:S(2)}, u32[]{:S(2)}) collective-permute-start(f32[4,64,512]{2,1,0:T(8,128)S(1)} %get-tuple-element.32), channel_id=1, source_target_pairs={{0,8},{8,16},{16,24},{24,32},{32,40},{40,48},{48,56},{56,64},{64,7... | collective-permute-start | bytes 1572872 | tf_op jit(solution)/shard_map/ppermute | solution.py:196
  3.7 2.6 %collective-permute-start.3 = (f32[4,64,512]{2,1,0:T(8,128)S(1)}, f32[4,64,512]{2,1,0:T(8,128)S(1)}, u32[]{:S(2)}, u32[]{:S(2)}) collective-permute-start(f32[4,64,512]{2,1,0:T(8,128)S(1)} %get-tuple-element.33), channel_id=1, source_target_pairs={{8,0},{16,8},{24,16},{32,24},{40,32},{48,40},{56,48},{64,56},{72,6... | collective-permute-start | bytes 1572872 | tf_op jit(solution)/shard_map/ppermute | solution.py:196
  6.2 0.0 collective-permute-start
  6.2 3.0 %collective-permute-start.1 = (f32[16,8,512]{2,1,0:T(8,128)S(1)}, f32[16,8,512]{2,1,0:T(8,128)S(1)}, u32[]{:S(2)}, u32[]{:S(2)}) collective-permute-start(f32[16,8,512]{2,1,0:T(8,128)S(1)} %get-tuple-element.27), channel_id=1, source_target_pairs={{1,0},{2,1},{3,2},{4,3},{5,4},{6,5},{7,6},{0,7},{9,8},{10,9},{11,1... | collective-permute-start | bytes 786440 | tf_op jit(solution)/shard_map/ppermute | solution.py:201
  9.2 0.0 copy-done
  9.2 0.0 copy-done.1
  9.2 0.0 copy-done.2
  9.2 3.7 %middle.1 = (f32[32,64,512]{2,1,0:T(8,128)S(1)}, f32[32,64,512]{2,1,0:T(8,128)S(1)}, f32[32,64,512]{2,1,0:T(8,128)S(1)}, f32[32,64,512]{2,1,0:T(8,128)S(1)}, f32[32,64,512]{2,1,0:T(8,128)S(1)}) custom-call(f32[32,64,512]{2,1,0:T(8,128)S(1)} %copy-done, f32[32,64,512]{2,1,0:T(8,128)S(1)} %copy-done.1, f32[32,64,512]{2,1,0:T(8,128)S(1)} %copy-done.2), custom_call_target="tpu_custom_call" | custom-call | flops 41943040 | bytes 16777216 | tf_op jit(solution)/shard_map/middle/pallas_call | solution.py:349
  12.9 0.4 %collective-permute-done.from_prev = f32[16,8,512]{2,1,0:T(8,128)S(1)} collective-permute-done((f32[16,8,512]{2,1,0:T(8,128)S(1)}, f32[16,8,512]{2,1,0:T(8,128)S(1)}, u32[]{:S(2)}, u32[]{:S(2)}) %collective-permute-start) | collective-permute-done | bytes 262176 | tf_op jit(solution)/shard_map/ppermute | solution.py:201
  13.3 0.0 collective-permute-done.1.from_next
  13.3 0.2 halo.1
  13.5 0.1 collective-permute-start.4
  13.5 4.1 %collective-permute-start.5 = (f32[2,8,512]{2,1,0:T(8,128)S(1)}, f32[2,8,512]{2,1,0:T(8,128)S(1)}, u32[]{:S(2)}, u32[]{:S(2)}) collective-permute-start(f32[2,8,512]{2,1,0:T(8,128)S(1)} %get-tuple-element.35), channel_id=1, source_target_pairs={{8,0},{16,8},{24,16},{32,24},{40,32},{48,40},{56,48},{64,56},{72,6... | collective-permute-start | bytes 98312 | tf_op jit(solution)/shard_map/ppermute | solution.py:196
  17.7 5.1 %inner.1 = (f32[32,64,512]{2,1,0:T(8,128)}, f32[32,64,512]{2,1,0:T(8,128)S(1)}, f32[4,24,512]{2,1,0:T(8,128)S(1)}, f32[4,24,512]{2,1,0:T(8,128)S(1)}, f32[4,24,5...) custom-call(f32[32,64,512]{2,1,0:T(8,128)S(1)} %copy-done, f32[32,64,512]{2,1,0:T(8,128)S(1)} %copy-done.1, ...), custom_call_target="tpu_custom_call" | custom-call | flops 41943040 | bytes 16777216 | tf_op jit(solution)/shard_map/inner/pallas_call | solution.py:441
  22.8 0.0 collective-permute-done.4.corner_out
  22.8 0.0 collective-permute-done.5.corner_back
  22.8 0.0 collective-permute-done.2.got_out
  22.8 0.0 collective-permute-done.3.got_back
  22.8 1.9 %outer.1 = f32[32,64,512]{2,1,0:T(8,128)} custom-call(f32[32,64,512]{2,1,0:T(8,128)S(1)} %copy-done, f32[32,64,512]{2,1,0:T(8,128)S(1)} %copy-done.1, f32[32,64,512]{2,1,0:T(8,128)S(1)} %copy-done.2, f32[32,8,512]{2,1,0:T(8,128)S(1)} %get-tuple-element.29.eh, f32[32,8,512]{2,1,0:T(8,128)S(1)} %get-tuple-element.30.mh, ...), custom_call_target="tpu_custom_call", output_to_operand_aliasing={{}: (21, {})} | custom-call | tf_op jit(solution)/shard_map/outer/pallas_call | solution.py:510
Async XLA Ops:
  0.0 9.2 %copy-start = (f32[32,64,512]{2,1,0:T(8,128)S(1)}, f32[32,64,512]{2,1,0:T(8,128)}, u32[]{:S(2)}) copy-start(f32[32,64,512]{2,1,0:T(8,128)} %e.7) | copy-start | bytes 12582916
  0.0 9.2 %copy-start.1 = (f32[32,64,512]{2,1,0:T(8,128)S(1)}, f32[32,64,512]{2,1,0:T(8,128)}, u32[]{:S(2)}) copy-start(f32[32,64,512]{2,1,0:T(8,128)} %m.7) | copy-start | bytes 12582916
  0.0 9.2 %copy-start.2 = (f32[32,64,512]{2,1,0:T(8,128)S(1)}, f32[32,64,512]{2,1,0:T(8,128)}, u32[]{:S(2)}) copy-start(f32[32,64,512]{2,1,0:T(8,128)} %r.7) | copy-start | bytes 12582916
  2.0 20.8 %collective-permute-start.2 = (f32[4,64,512]{2,1,0:T(8,128)S(1)}, f32[4,64,512]{2,1,0:T(8,128)S(1)}, u32[]{:S(2)}, u32[]{:S(2)}) collective-permute-start(f32[4,64,512]{2,1,0:T(8,128)S(1)} %get-tuple-element.32), channel_id=1, source_target_pairs={{0,8},{8,16},{16,24},{24,32},{32,40},{40,48},{48,56},{56,64},{64,7... | collective-permute-start | bytes 1572872 | tf_op jit(solution)/shard_map/ppermute | solution.py:196
  3.7 19.2 %collective-permute-start.3 = (f32[4,64,512]{2,1,0:T(8,128)S(1)}, f32[4,64,512]{2,1,0:T(8,128)S(1)}, u32[]{:S(2)}, u32[]{:S(2)}) collective-permute-start(f32[4,64,512]{2,1,0:T(8,128)S(1)} %get-tuple-element.33), channel_id=1, source_target_pairs={{8,0},{16,8},{24,16},{32,24},{40,32},{48,40},{56,48},{64,56},{72,6... | collective-permute-start | bytes 1572872 | tf_op jit(solution)/shard_map/ppermute | solution.py:196
  6.2 7.0 %collective-permute-start = (f32[16,8,512]{2,1,0:T(8,128)S(1)}, f32[16,8,512]{2,1,0:T(8,128)S(1)}, u32[]{:S(2)}, u32[]{:S(2)}) collective-permute-start(f32[16,8,512]{2,1,0:T(8,128)S(1)} %get-tuple-element.26), channel_id=1, source_target_pairs={{0,1},{1,2},{2,3},{3,4},{4,5},{5,6},{6,7},{7,0},{8,9},{9,10},{10,1... | collective-permute-start | bytes 786440 | tf_op jit(solution)/shard_map/ppermute | solution.py:201
  6.2 7.0 %collective-permute-start.1 = (f32[16,8,512]{2,1,0:T(8,128)S(1)}, f32[16,8,512]{2,1,0:T(8,128)S(1)}, u32[]{:S(2)}, u32[]{:S(2)}) collective-permute-start(f32[16,8,512]{2,1,0:T(8,128)S(1)} %get-tuple-element.27), channel_id=1, source_target_pairs={{1,0},{2,1},{3,2},{4,3},{5,4},{6,5},{7,6},{0,7},{9,8},{10,9},{11,1... | collective-permute-start | bytes 786440 | tf_op jit(solution)/shard_map/ppermute | solution.py:201
  13.5 9.3 %collective-permute-start.4 = (f32[2,8,512]{2,1,0:T(8,128)S(1)}, f32[2,8,512]{2,1,0:T(8,128)S(1)}, u32[]{:S(2)}, u32[]{:S(2)}) collective-permute-start(f32[2,8,512]{2,1,0:T(8,128)S(1)} %get-tuple-element.34), channel_id=1, source_target_pairs={{0,8},{8,16},{16,24},{24,32},{32,40},{40,48},{48,56},{56,64},{64,7... | collective-permute-start | bytes 98312 | tf_op jit(solution)/shard_map/ppermute | solution.py:196
  13.5 9.3 %collective-permute-start.5 = (f32[2,8,512]{2,1,0:T(8,128)S(1)}, f32[2,8,512]{2,1,0:T(8,128)S(1)}, u32[]{:S(2)}, u32[]{:S(2)}) collective-permute-start(f32[2,8,512]{2,1,0:T(8,128)S(1)} %get-tuple-element.35), channel_id=1, source_target_pairs={{8,0},{16,8},{24,16},{32,24},{40,32},{48,40},{56,48},{64,56},{72,6... | collective-permute-start | bytes 98312 | tf_op jit(solution)/shard_map/ppermute | solution.py:196

commit v6 on v5

--- a/solution.py
+++ b/solution.py
@@ -468,6 +468,7 @@
     late = pl.ds(unsent(nx), nx - 2 - unsent(nx))
     writes = [pltpu.make_async_copy(second.at[late], out_hbm.at[late], sems.at[4])]
     writes[0].start()
+    sides = []
     for side, (got, corner) in enumerate(((got_out, corner_out), (got_back, corner_back))):
         low = sends_up(side == 1)
         there = jnp.where(low, has_prev("space"), has_next("space"))
@@ -475,7 +476,7 @@
         def at(q, low=low):
             return jnp.where(low, q, nx - 1 - q)
 
-        def place(name, q, j, got=got, corner=corner, low=low, at=at):
+        def place(name, q, j, got=got, corner=corner, low=low, at=at, side=side):
             if name in own:
                 if q >= 0:
                     return (strips[name], at(q), 0) if j == n else (own[name], at(q), ROWS * j)
@@ -483,19 +484,26 @@
                     return corner, corner_at[name], 0
                 return got, got_at[name, q], ROWS * j
             if q <= 0:
-                return made[name], 1 + q, ROWS * j
+                return made[name], 2 * side + 1 + q, ROWS * j
             i = jnp.where(low, q, nx - 2 - q) if name == "cx" else at(q)
             end = jnp.where(low, q - 1, 3 - q if name == "cx" else 4 - q)
             return made_place(middles, ends, n, name, i, end, j)
 
-        slab = Slab(place, lambda name, q: (rings[name], q % 2), ny, nz, mask)
+        slab = Slab(place, lambda name, q, side=side: (rings[name], 2 * side + q % 2), ny, nz, mask)
         keep = jnp.broadcast_to(jnp.where(there, 1, 0), (ROWS, LANES)) == 1
-        run(slab.load(-1, range(n + 1), TURNED1), slab.load(0, range(n + 1), TURNED1))
-        run(slab.load(1, range(n + 1), TURNED2))
-        run(slab.first(-1, range(n), keep=keep, e_before=False))
-        run(slab.first(0, range(n + 1)))
-        run(slab.load(0, range(n + 1), TURNED2))
-        for q in (0, 1):
+        sides.append((slab, keep, at))
+
+    def both(call):
+        run(*(call(slab, keep) for slab, keep, _ in sides))
+
+    both(lambda slab, _: slab.load(-1, range(n + 1), TURNED1))
+    both(lambda slab, _: slab.load(0, range(n + 1), TURNED1))
+    both(lambda slab, _: slab.load(1, range(n + 1), TURNED2))
+    both(lambda slab, keep: slab.first(-1, range(n), keep=keep, e_before=False))
+    both(lambda slab, _: slab.first(0, range(n + 1)))
+    both(lambda slab, _: slab.load(0, range(n + 1), TURNED2))
+    for q in (0, 1):
+        for side, (slab, _, at) in enumerate(sides):
             run(slab.second(q, out, 2 * side + q))
             c = pltpu.make_async_copy(out.at[2 * side + q], out_hbm.at[at(q)], sems.at[2 * side + q])
             c.start()
@@ -513,10 +521,10 @@
         in_specs=[VMEM] * len(args) + [HBM],
         out_specs=HBM,
         input_output_aliases={len(args): 0},
-        scratch_shapes=[pltpu.VMEM((2, ny + ROWS, nz), F32)] * len(MADE)
-        + [pltpu.VMEM(turned_shape(2, ny, nz), F32)] * 4
+        scratch_shapes=[pltpu.VMEM((4, ny + ROWS, nz), F32)] * len(MADE)
+        + [pltpu.VMEM(turned_shape(4, ny, nz), F32)] * 4
         + [pltpu.VMEM((4, ny, nz), F32), pltpu.SemaphoreType.DMA((5,))],
-        compiler_params=pltpu.CompilerParams(vmem_limit_bytes=6 * 2**20),
+        compiler_params=pltpu.CompilerParams(vmem_limit_bytes=8 * 2**20),
         name="outer",
     )(*args, out)
 

time: 24.8 us -> 24.8 us (level)
  no operation moved by 1% of the time
where the time goes in v6:
time: 24.8 us; the launch traced here: 24.7 us
  Pallas kernels  12.9 us (52%)
  starting transfers between devices  11.4 us (46%)
  waiting for transfers between devices  0.4 us (2%)
    ppermute x4, starting transfers between devices, along_space(): lax.ppermute(x, ('space', 'member'), [(b, a) for a, b in hops] if back el...  8.4 us
    pallas_call x1, Pallas kernels, inner(): pl.pallas_call(inner_kernel, out_shape=[jax.ShapeDtypeStruct((nx, ny, nz)...  5.13 us
    pallas_call x1, Pallas kernels, middle(): pl.pallas_call(middle_kernel, out_shape=[jax.ShapeDtypeStruct((nx, ny, nz...  3.65 us
    ppermute x2, starting transfers between devices, along_member(): lax.ppermute(x, 'member', [((i + 1) % n, i) if back else (i, (i + 1) % n)...  2.96 us
    pallas_call x1, Pallas kernels, send(): pl.pallas_call(send_kernel, out_shape=[rows, rows, planes, planes], in_sp...  2.02 us
    pallas_call x1, Pallas kernels, outer(): pl.pallas_call(outer_kernel, out_shape=jax.ShapeDtypeStruct((nx, ny, nz),...  1.87 us
  transfers between devices with their start and end apart: 6, of which 1 were waited for; matrix products, arithmetic and copies ran while one was open for 0% of the time, Pallas kernels for 36%

profile of v6, /device:TPU:64, one launch (start us, length us, event | category | flops | bytes accessed | tf_op | source)
XLA Modules:
  0.0 24.7 jit_solution(12334706114799620237)
XLA Ops:
  0.0 0.0 copy-start
  0.0 0.0 copy-start.1
  0.0 0.0 copy-start.2
  0.0 2.0 %send.1 = (f32[16,8,512]{2,1,0:T(8,128)S(1)}, f32[16,8,512]{2,1,0:T(8,128)S(1)}, f32[4,64,512]{2,1,0:T(8,128)S(1)}, f32[4,64,512]{2,1,0:T(8,128)S(1)}) custom-call(f32[32,64,512]{2,1,0:T(8,128)} %e.7, f32[32,64,512]{2,1,0:T(8,128)} %m.7, f32[32,64,512]{2,1,0:T(8,128)} %r.7), custom_call_target="tpu_custom_call" | custom-call | tf_op jit(solution)/shard_map/send/pallas_call | solution.py:285
  2.0 1.6 %collective-permute-start.2 = (f32[4,64,512]{2,1,0:T(8,128)S(1)}, f32[4,64,512]{2,1,0:T(8,128)S(1)}, u32[]{:S(2)}, u32[]{:S(2)}) collective-permute-start(f32[4,64,512]{2,1,0:T(8,128)S(1)} %get-tuple-element.32), channel_id=1, source_target_pairs={{0,8},{8,16},{16,24},{24,32},{32,40},{40,48},{48,56},{56,64},{64,7... | collective-permute-start | bytes 1572872 | tf_op jit(solution)/shard_map/ppermute | solution.py:196
  3.7 2.6 %collective-permute-start.3 = (f32[4,64,512]{2,1,0:T(8,128)S(1)}, f32[4,64,512]{2,1,0:T(8,128)S(1)}, u32[]{:S(2)}, u32[]{:S(2)}) collective-permute-start(f32[4,64,512]{2,1,0:T(8,128)S(1)} %get-tuple-element.33), channel_id=1, source_target_pairs={{8,0},{16,8},{24,16},{32,24},{40,32},{48,40},{56,48},{64,56},{72,6... | collective-permute-start | bytes 1572872 | tf_op jit(solution)/shard_map/ppermute | solution.py:196
  6.2 0.0 collective-permute-start
  6.2 3.0 %collective-permute-start.1 = (f32[16,8,512]{2,1,0:T(8,128)S(1)}, f32[16,8,512]{2,1,0:T(8,128)S(1)}, u32[]{:S(2)}, u32[]{:S(2)}) collective-permute-start(f32[16,8,512]{2,1,0:T(8,128)S(1)} %get-tuple-element.27), channel_id=1, source_target_pairs={{1,0},{2,1},{3,2},{4,3},{5,4},{6,5},{7,6},{0,7},{9,8},{10,9},{11,1... | collective-permute-start | bytes 786440 | tf_op jit(solution)/shard_map/ppermute | solution.py:201
  9.2 0.0 copy-done
  9.2 0.0 copy-done.1
  9.2 0.0 copy-done.2
  9.2 3.7 %middle.1 = (f32[32,64,512]{2,1,0:T(8,128)S(1)}, f32[32,64,512]{2,1,0:T(8,128)S(1)}, f32[32,64,512]{2,1,0:T(8,128)S(1)}, f32[32,64,512]{2,1,0:T(8,128)S(1)}, f32[32,64,512]{2,1,0:T(8,128)S(1)}) custom-call(f32[32,64,512]{2,1,0:T(8,128)S(1)} %copy-done, f32[32,64,512]{2,1,0:T(8,128)S(1)} %copy-done.1, f32[32,64,512]{2,1,0:T(8,128)S(1)} %copy-done.2), custom_call_target="tpu_custom_call" | custom-call | flops 41943040 | bytes 16777216 | tf_op jit(solution)/shard_map/middle/pallas_call | solution.py:349
  12.9 0.4 %collective-permute-done.from_prev = f32[16,8,512]{2,1,0:T(8,128)S(1)} collective-permute-done((f32[16,8,512]{2,1,0:T(8,128)S(1)}, f32[16,8,512]{2,1,0:T(8,128)S(1)}, u32[]{:S(2)}, u32[]{:S(2)}) %collective-permute-start) | collective-permute-done | bytes 262176 | tf_op jit(solution)/shard_map/ppermute | solution.py:201
  13.3 0.0 collective-permute-done.1.from_next
  13.3 0.2 halo.1
  13.5 0.1 collective-permute-start.4
  13.5 4.1 %collective-permute-start.5 = (f32[2,8,512]{2,1,0:T(8,128)S(1)}, f32[2,8,512]{2,1,0:T(8,128)S(1)}, u32[]{:S(2)}, u32[]{:S(2)}) collective-permute-start(f32[2,8,512]{2,1,0:T(8,128)S(1)} %get-tuple-element.35), channel_id=1, source_target_pairs={{8,0},{16,8},{24,16},{32,24},{40,32},{48,40},{56,48},{64,56},{72,6... | collective-permute-start | bytes 98312 | tf_op jit(solution)/shard_map/ppermute | solution.py:196
  17.7 5.1 %inner.1 = (f32[32,64,512]{2,1,0:T(8,128)}, f32[32,64,512]{2,1,0:T(8,128)S(1)}, f32[4,24,512]{2,1,0:T(8,128)S(1)}, f32[4,24,512]{2,1,0:T(8,128)S(1)}, f32[4,24,5...) custom-call(f32[32,64,512]{2,1,0:T(8,128)S(1)} %copy-done, f32[32,64,512]{2,1,0:T(8,128)S(1)} %copy-done.1, ...), custom_call_target="tpu_custom_call" | custom-call | flops 41943040 | bytes 16777216 | tf_op jit(solution)/shard_map/inner/pallas_call | solution.py:441
  22.8 0.0 collective-permute-done.4.corner_out
  22.8 0.0 collective-permute-done.5.corner_back
  22.8 0.0 collective-permute-done.2.got_out
  22.8 0.0 collective-permute-done.3.got_back
  22.8 1.9 %outer.1 = f32[32,64,512]{2,1,0:T(8,128)} custom-call(f32[32,64,512]{2,1,0:T(8,128)S(1)} %copy-done, f32[32,64,512]{2,1,0:T(8,128)S(1)} %copy-done.1, f32[32,64,512]{2,1,0:T(8,128)S(1)} %copy-done.2, f32[32,8,512]{2,1,0:T(8,128)S(1)} %get-tuple-element.29.eh, f32[32,8,512]{2,1,0:T(8,128)S(1)} %get-tuple-element.30.mh, ...), custom_call_target="tpu_custom_call", output_to_operand_aliasing={{}: (21, {})} | custom-call | tf_op jit(solution)/shard_map/outer/pallas_call | solution.py:518
Async XLA Ops:
  0.0 9.2 %copy-start = (f32[32,64,512]{2,1,0:T(8,128)S(1)}, f32[32,64,512]{2,1,0:T(8,128)}, u32[]{:S(2)}) copy-start(f32[32,64,512]{2,1,0:T(8,128)} %e.7) | copy-start | bytes 12582916
  0.0 9.2 %copy-start.1 = (f32[32,64,512]{2,1,0:T(8,128)S(1)}, f32[32,64,512]{2,1,0:T(8,128)}, u32[]{:S(2)}) copy-start(f32[32,64,512]{2,1,0:T(8,128)} %m.7) | copy-start | bytes 12582916
  0.0 9.2 %copy-start.2 = (f32[32,64,512]{2,1,0:T(8,128)S(1)}, f32[32,64,512]{2,1,0:T(8,128)}, u32[]{:S(2)}) copy-start(f32[32,64,512]{2,1,0:T(8,128)} %r.7) | copy-start | bytes 12582916
  2.0 20.8 %collective-permute-start.2 = (f32[4,64,512]{2,1,0:T(8,128)S(1)}, f32[4,64,512]{2,1,0:T(8,128)S(1)}, u32[]{:S(2)}, u32[]{:S(2)}) collective-permute-start(f32[4,64,512]{2,1,0:T(8,128)S(1)} %get-tuple-element.32), channel_id=1, source_target_pairs={{0,8},{8,16},{16,24},{24,32},{32,40},{40,48},{48,56},{56,64},{64,7... | collective-permute-start | bytes 1572872 | tf_op jit(solution)/shard_map/ppermute | solution.py:196
  3.7 19.2 %collective-permute-start.3 = (f32[4,64,512]{2,1,0:T(8,128)S(1)}, f32[4,64,512]{2,1,0:T(8,128)S(1)}, u32[]{:S(2)}, u32[]{:S(2)}) collective-permute-start(f32[4,64,512]{2,1,0:T(8,128)S(1)} %get-tuple-element.33), channel_id=1, source_target_pairs={{8,0},{16,8},{24,16},{32,24},{40,32},{48,40},{56,48},{64,56},{72,6... | collective-permute-start | bytes 1572872 | tf_op jit(solution)/shard_map/ppermute | solution.py:196
  6.2 7.0 %collective-permute-start = (f32[16,8,512]{2,1,0:T(8,128)S(1)}, f32[16,8,512]{2,1,0:T(8,128)S(1)}, u32[]{:S(2)}, u32[]{:S(2)}) collective-permute-start(f32[16,8,512]{2,1,0:T(8,128)S(1)} %get-tuple-element.26), channel_id=1, source_target_pairs={{0,1},{1,2},{2,3},{3,4},{4,5},{5,6},{6,7},{7,0},{8,9},{9,10},{10,1... | collective-permute-start | bytes 786440 | tf_op jit(solution)/shard_map/ppermute | solution.py:201
  6.2 7.0 %collective-permute-start.1 = (f32[16,8,512]{2,1,0:T(8,128)S(1)}, f32[16,8,512]{2,1,0:T(8,128)S(1)}, u32[]{:S(2)}, u32[]{:S(2)}) collective-permute-start(f32[16,8,512]{2,1,0:T(8,128)S(1)} %get-tuple-element.27), channel_id=1, source_target_pairs={{1,0},{2,1},{3,2},{4,3},{5,4},{6,5},{7,6},{0,7},{9,8},{10,9},{11,1... | collective-permute-start | bytes 786440 | tf_op jit(solution)/shard_map/ppermute | solution.py:201
  13.5 9.3 %collective-permute-start.4 = (f32[2,8,512]{2,1,0:T(8,128)S(1)}, f32[2,8,512]{2,1,0:T(8,128)S(1)}, u32[]{:S(2)}, u32[]{:S(2)}) collective-permute-start(f32[2,8,512]{2,1,0:T(8,128)S(1)} %get-tuple-element.34), channel_id=1, source_target_pairs={{0,8},{8,16},{16,24},{24,32},{32,40},{40,48},{48,56},{56,64},{64,7... | collective-permute-start | bytes 98312 | tf_op jit(solution)/shard_map/ppermute | solution.py:196
  13.5 9.3 %collective-permute-start.5 = (f32[2,8,512]{2,1,0:T(8,128)S(1)}, f32[2,8,512]{2,1,0:T(8,128)S(1)}, u32[]{:S(2)}, u32[]{:S(2)}) collective-permute-start(f32[2,8,512]{2,1,0:T(8,128)S(1)} %get-tuple-element.35), channel_id=1, source_target_pairs={{8,0},{16,8},{24,16},{32,24},{40,32},{48,40},{56,48},{64,56},{72,6... | collective-permute-start | bytes 98312 | tf_op jit(solution)/shard_map/ppermute | solution.py:196
